TPU v7x, 32 devices: a whole 2x2x4 slice. The times are simulated.
32 devices in a mesh: pipe: 2 (over y), patch: 8 (over z, x), hour: 2 (over core).
Axes of the slice: x: 2, y: 2, z: 4, core: 2. Of those that a mesh axis runs over, the one named last changes fastest.
Arguments:
- inputs: bfloat16 [2, 128, 32, 512], P(None, 'patch', 'hour'), may hold values from -6 to 6
- visibility: int32 [2, 2], replicated, may hold values from 0 to 1, all different within a row
- norm_gains: float32 [2, 3, 512], P('pipe'), may hold values from 0.1 to 1.9
- scales: float32 [2, 2, 8], P('pipe'), may hold values from 2 to 12
- mixer_in: bfloat16 [2, 2, 512, 1536], P('pipe'), may hold values from -0.25 to 0.25
- mixer_out: bfloat16 [2, 2, 512, 512], P('pipe'), may hold values from -0.25 to 0.25
- expand_weight: bfloat16 [2, 512, 2048], P('pipe'), may hold values from -0.25 to 0.25
- reduce_weight: bfloat16 [2, 2048, 512], P('pipe'), may hold values from -0.125 to 0.125
Outputs:
- outputs: bfloat16 [2, 128, 32, 512], P(None, 'patch', 'hour')
Inputs may be any that keep to these rules, and one draw needn't show every extreme that they name: `visibility`: row b lists 2 different key blocks of 64 patches for query block b; every block is listed in some row.
All inputs are finite; a program needn't handle non-finite values.
Results may differ from a plain program's by a relative error of at most 0.023.
Values may be sent and summed in bfloat16 or wider, within the bound.
No kernel may reach another device: no remote copies, remote signals or barrier semaphores. Data moves between devices by JAX's collectives and lax.ppermute only.
A program may use at most 64 MiB of HBM per device.

v0:
```python
import functools

import jax
import jax.numpy as jnp
from jax import lax
from jax.experimental import pallas as pl
from jax.experimental.pallas import tpu as pltpu
from jax.sharding import PartitionSpec as P

HEADS = 8
HEAD_DIM = 64
PB = 64
LOG2E = 1.4426950408889634


def row_norm(x, gain):
    factor = lax.rsqrt(jnp.mean(x * x, axis=-1, keepdims=True) + 1e-05)
    return (x * factor * gain).astype(jnp.bfloat16)


def matmul(a, b):
    return jnp.dot(a, b, preferred_element_type=jnp.float32)


def same_head():
    rows = lax.broadcasted_iota(jnp.int32, (256, 256), 0) // HEAD_DIM
    cols = lax.broadcasted_iota(jnp.int32, (256, 256), 1) // HEAD_DIM
    return jnp.where(rows == cols, 1.0, 0.0).astype(jnp.bfloat16)


def head_factor(values, group):
    squares = (values * values).astype(jnp.bfloat16)
    halves = [
        matmul(squares[:, start : start + 256], group) for start in range(0, values.shape[1], 256)
    ]
    sums = jnp.concatenate(halves, axis=1)
    return lax.rsqrt(sums * (1.0 / HEAD_DIM) + 1e-06)


def attention_update(x, more, gain, scale_of, w_in, w_out, mask):
    width = x.shape[1]
    normed = row_norm(x, gain)
    seen = jnp.concatenate([normed] + [row_norm(t, gain) for t in more], axis=0)
    group = same_head()
    head = lax.broadcasted_iota(jnp.int32, (1, width), 1) // HEAD_DIM
    scale = jnp.zeros((1, width), jnp.float32)
    for n in range(HEADS):
        scale = jnp.where(head == n, scale_of(n) * (LOG2E / HEAD_DIM), scale)
    q = matmul(normed, w_in[:, :width])
    k = matmul(seen, w_in[:, width : 2 * width])
    v = matmul(seen, w_in[:, 2 * width :]).astype(jnp.bfloat16)
    q = (q * head_factor(q, group) * scale).astype(jnp.bfloat16)
    k = (k * head_factor(k, group)).astype(jnp.bfloat16)
    pair = 2 * HEAD_DIM
    first = lax.broadcasted_iota(jnp.int32, (1, pair), 1) < HEAD_DIM
    low = jnp.where(first, 1.0, 0.0).astype(jnp.bfloat16)
    high = jnp.where(first, 0.0, 1.0).astype(jnp.bfloat16)
    low_all = jnp.broadcast_to(low, (k.shape[0], pair))
    high_all = jnp.broadcast_to(high, (k.shape[0], pair))
    parts = []
    for start in range(0, width, pair):
        q2, k2, v2 = (t[:, start : start + pair] for t in (q, k, v))
        powers = []
        for side in (low, high):
            scores = lax.dot_general(
                q2 * side, k2, (((1,), (1,)), ((), ())), preferred_element_type=jnp.float32
            )
            powers.append(jnp.exp2(scores).astype(jnp.bfloat16) * mask)
        powers = jnp.concatenate(powers, axis=1)
        upper = jnp.concatenate([v2 * low, low_all], axis=1)
        lower = jnp.concatenate([v2 * high, high_all], axis=1)
        sums = matmul(powers, jnp.concatenate([upper, lower], axis=0))
        parts.append((sums[:, :pair] / sums[:, pair:]).astype(jnp.bfloat16))
    return matmul(jnp.concatenate(parts, axis=1), w_out[...])


def rounded(x):
    return x.astype(jnp.bfloat16).astype(jnp.float32)


def digits(shape, dimension, *bases):
    index = lax.broadcasted_iota(jnp.int32, shape, dimension)
    out = []
    for base in bases:
        out.append(index % base)
        index = index // base
    return out + [index]


def at_work(place_ref, step, micro):
    number = step - place_ref[0]
    return jnp.logical_and(number >= 0, number < micro)


def time_kernel(sizes, step, micro, place_ref, *refs):
    shards, peers, patches, hl = sizes
    given = peers if step < micro else 0
    came = peers if step > 0 else 0
    input_refs, refs = refs[:given], refs[given:]
    came_refs, refs = refs[:came], refs[came:]
    (gain_ref, scale_ref, w_in_ref, w_out_ref), refs = refs[:4], refs[4:]
    y_refs, refs = refs[:shards], refs[shards:]
    x_ref = refs[0]
    rows = x_ref.shape[0] // peers

    @pl.when(at_work(place_ref, step, micro))
    def _():
        if given:

            @pl.when(place_ref[0] == 0)
            def _():
                late, patch, offset = digits((rows, rows), 0, hl, patches)
                source = lax.broadcasted_iota(jnp.int32, (rows, rows), 1)
                wanted = (patch * shards + (offset ^ place_ref[1])) * hl + late
                order = jnp.where(wanted == source, 1.0, 0.0).astype(jnp.bfloat16)
                for j, ref in enumerate(input_refs):
                    moved = matmul(order, ref[step]).astype(jnp.bfloat16)
                    x_ref[j * rows : (j + 1) * rows, :] = moved

        if came:

            @pl.when(place_ref[0] != 0)
            def _():
                for j, ref in enumerate(came_refs):
                    x_ref[j * rows : (j + 1) * rows, :] = ref[...]

        x = x_ref[...].astype(jnp.float32)
        mine = digits((rows, rows * peers), 0, hl, patches)[1]
        theirs = digits((rows, rows * peers), 1, hl, patches)[1]
        mask = jnp.where(mine == theirs, 1.0, 0.0).astype(jnp.bfloat16)
        update = attention_update(
            x[:rows],
            [x[rows:]],
            gain_ref[0, 0:1, :],
            lambda n: scale_ref[0, 0, n],
            w_in_ref.at[0, 0],
            w_out_ref.at[0, 0],
            mask,
        )
        y = (x[:rows] + update).astype(jnp.bfloat16)
        size = rows // shards
        for k in range(shards):
            y_refs[k][...] = y[k * size : (k + 1) * size]


def patch_kernel(sizes, step, micro, place_ref, seen_ref, *refs):
    slow, _, patches, hl = sizes
    fast = len(refs) - 6 - slow
    x_refs, (gain_ref, scale_ref, w_in_ref, w_out_ref, up_ref, down_ref), y_refs = (
        refs[:fast],
        refs[fast : fast + 6],
        refs[fast + 6 :],
    )

    @pl.when(at_work(place_ref, step, micro))
    def _():
        xs = [x_ref[...].astype(jnp.float32) for x_ref in x_refs]
        x = xs[0]
        rows = x.shape[0]
        shape = (rows, rows * fast)

        def block_and_hour(dimension):
            late, patch, offset, other = digits(shape, dimension, hl, patches, slow)
            shard = (offset ^ place_ref[1]) * fast + (other ^ place_ref[2])
            return (shard * patches + patch) // PB, late

        query_block, query_hour = block_and_hour(0)
        key_block, key_hour = block_and_hour(1)
        seen = None
        for kv in range(seen_ref.shape[1]):
            chosen = jnp.full(shape, seen_ref[0, kv], jnp.int32)
            for b in range(1, seen_ref.shape[0]):
                chosen = jnp.where(query_block == b, seen_ref[b, kv], chosen)
            hit = jnp.where(chosen == key_block, 1.0, 0.0)
            seen = hit if seen is None else jnp.maximum(seen, hit)
        mask = jnp.where(query_hour == key_hour, seen, 0.0).astype(jnp.bfloat16)
        update = attention_update(
            x,
            xs[1:],
            gain_ref[0, 1:2, :],
            lambda n: scale_ref[0, 1, n],
            w_in_ref.at[0, 1],
            w_out_ref.at[0, 1],
            mask,
        )
        x = rounded(x + update)
        normed = row_norm(x, gain_ref[0, 2:3, :])
        total = x
        chunk = 512
        for start in range(0, up_ref.shape[2], chunk):
            u = matmul(normed, up_ref[0, :, start : start + chunk])
            bent = jnp.tanh(u * (0.7978845608028654 + 0.035677408136300125 * (u * u)))
            hidden = (0.5 * u * (1.0 + bent)).astype(jnp.bfloat16)
            total = total + matmul(hidden, down_ref[0, start : start + chunk, :])
        y = total.astype(jnp.bfloat16)
        size = rows // slow
        for k in range(slow):
            y_refs[k][...] = y[k * size : (k + 1) * size]


def final_kernel(sizes, micro, place_ref, *refs):
    shards, _, patches, hl = sizes
    y_ref = refs[-1]
    rows = shards * patches * hl
    late, shard, patch = digits((rows, rows), 0, hl, shards)
    source = lax.broadcasted_iota(jnp.int32, (rows, rows), 1)
    wanted = ((shard ^ place_ref[1]) * patches + patch) * hl + late
    order = jnp.where(wanted == source, 1.0, 0.0).astype(jnp.bfloat16)
    for hops in range(len(refs) // micro):

        @pl.when(place_ref[0] == hops)
        def _():
            for m in range(micro):
                y_ref[m] = matmul(order, refs[hops * micro + m][...]).astype(jnp.bfloat16)


VMEM = pl.BlockSpec(memory_space=pltpu.VMEM)
SMEM = pl.BlockSpec(memory_space=pltpu.SMEM)
PARAMS = pltpu.CompilerParams(vmem_limit_bytes=32 << 20)
COST = pl.CostEstimate(flops=5 << 30, bytes_accessed=1 << 20, transcendentals=1 << 20)


def blocks_of(count, rows, width):
    return [jax.ShapeDtypeStruct((rows // count, width), jnp.bfloat16)] * count


def call_time(sizes, step, micro, place, given, came, gains, scales, w_in, w_out):
    rows, width = given[0].shape[1:] if given else came[0].shape
    xs = list(given) + list(came)
    return pl.pallas_call(
        functools.partial(time_kernel, sizes, step, micro),
        out_shape=blocks_of(sizes[0], rows, width),
        in_specs=[SMEM] + [VMEM] * len(xs) + [VMEM, SMEM, VMEM, VMEM],
        out_specs=[VMEM] * sizes[0],
        scratch_shapes=[pltpu.VMEM((rows * sizes[1], width), jnp.bfloat16)],
        compiler_params=PARAMS,
        cost_estimate=COST,
        name="time_attention",
    )(place, *xs, gains, scales, w_in, w_out)


def call_patch(sizes, step, micro, place, seen, xs, gains, scales, w_in, w_out, w_up, w_down):
    rows, width = xs[0].shape
    return pl.pallas_call(
        functools.partial(patch_kernel, sizes, step, micro),
        out_shape=blocks_of(sizes[0], rows, width),
        in_specs=[SMEM, SMEM] + [VMEM] * len(xs) + [VMEM, SMEM] + [VMEM] * 4,
        out_specs=[VMEM] * sizes[0],
        compiler_params=PARAMS,
        cost_estimate=COST,
        name="patch_attention_and_ffn",
    )(place, seen, *xs, gains, scales, w_in, w_out, w_up, w_down)


def call_final(sizes, place, shape, parts):
    micro, rows, width = shape
    return pl.pallas_call(
        functools.partial(final_kernel, sizes, micro),
        out_shape=jax.ShapeDtypeStruct((micro, rows, width), jnp.bfloat16),
        in_specs=[SMEM] + [VMEM] * len(parts),
        out_specs=VMEM,
        compiler_params=PARAMS,
        name="final_order",
    )(place, *parts)


def flipped(x, axis, k):
    return lax.ppermute(x, axis, [(s, s ^ k) for s in range(lax.axis_size(axis))])


def handed_on(x, k):
    pipes, shards = lax.axis_size("pipe"), lax.axis_size("patch")
    pairs = [
        (stage * shards + s, (stage + 1) % pipes * shards + (s ^ k))
        for stage in range(pipes)
        for s in range(shards)
    ]
    return lax.ppermute(x, ("pipe", "patch"), pairs)


def local(inputs, seen, gains, scales, w_in, w_out, w_up, w_down):
    shards = lax.axis_size("patch")
    peers = lax.axis_size("hour")
    pipes = lax.axis_size("pipe")
    micro, patches, hours, width = inputs.shape
    rows = patches * hours
    fast = 2
    slow = shards // fast
    sizes = (slow, peers, patches, hours // slow)
    shard = lax.axis_index("patch")
    place = jnp.stack([lax.axis_index("pipe"), lax.div(shard, fast), lax.rem(shard, fast)])
    order = sorted(range(slow), key=lambda k: (k < slow // 2, k))

    def with_others(x, axis, count):
        return [x] + [flipped(x, axis, j) for j in range(1, count)]

    def along_slow(blocks, send, first):
        got = {k: send(blocks[k], k * fast) for k in order if k >= first}
        return jnp.concatenate([got.get(k, blocks[k]) for k in range(slow)])

    def onward(x):
        return lax.ppermute(x, "pipe", [(s, (s + 1) % pipes) for s in range(pipes)])

    given = with_others(inputs.reshape(micro, rows, width), "hour", peers)
    came = []
    finished = []
    back = []
    for step in range(micro + pipes - 1):
        if step > 0:
            came = with_others(arrived, "hour", peers)
        now = given if step < micro else []
        mixed = call_time(sizes, step, micro, place, now, came, gains, scales, w_in, w_out)
        own = along_slow(mixed, lambda x, k: flipped(x, "patch", k), 1)
        spread = with_others(own, "patch", fast)
        if back:
            spread, back = lax.optimization_barrier((spread, back))
            finished[-1][1:] = back
        done = call_patch(
            sizes, step, micro, place, seen, spread, gains, scales, w_in, w_out, w_up, w_down
        )
        arrived = along_slow(done, handed_on, 0)
        back = []
        if step >= pipes - 1:
            for _ in range(1, pipes):
                back.append(onward(back[-1] if back else arrived))
            finished.append([arrived] + back)
    parts = [copies[hops] for hops in range(pipes) for copies in finished]
    return call_final(sizes, place, (micro, rows, width), parts).reshape(inputs.shape)


def solution(mesh):
    placed = (
        P(None, "patch", "hour", None),
        P(),
        P("pipe", None, None),
        P("pipe", None, None),
        P("pipe", None, None, None),
        P("pipe", None, None, None),
        P("pipe", None, None),
        P("pipe", None, None),
    )
    return jax.shard_map(
        local, mesh=mesh, in_specs=placed, out_specs=P(None, "patch", "hour", None), check_vma=False
    )
```

profile of v0, /device:TPU:0, one launch (start us, length us, event | category | flops | bytes accessed | tf_op | source)
XLA Modules:
  0.0 128.9 jit_solution(15577159805584820853)
XLA Ops:
  2.2 1.9 %copy-done = bf16[1,2,512,1536]{3,2,1,0:T(8,128)(2,1)S(1)} copy-done((bf16[1,2,512,1536]{3,2,1,0:T(8,128)(2,1)S(1)}, bf16[1,2,512,1536]{3,2,1,0:T(8,128)(2,1)}, u32[]{:S(2)}) %copy-start) | copy-done | bytes 3145752
  7.1 3.5 %time_attention.3 = (bf16[64,512]{1,0:T(8,128)(2,1)S(1)}, bf16[64,512]{1,0:T(8,128)(2,1)S(1)}, bf16[64,512]{1,0:T(8,128)(2,1)S(1)}, bf16[64,512]{1,0:T(8,128)(2,1)S(1)}) custom-call(s32[3]{0:T(128)S(1)} %pad_add_fusion.place_ref, bf16[2,256,512]{2,1,0:T(8,128)(2,1)S(1)} %bitcast.6, bf16[2,256,512]{2,1,0:T(8,128)(2,1)S(1)} %collective-permute-done.refs_1_, ...), custom_call_target="tpu_custom_call" | custom-call | flops 5368709120 | bytes 1048576 | tf_op jit(solution)/shard_map/time_attention/pallas_call | solution.py:230
  10.6 3.0 %collective-permute-start.1 = (bf16[64,512]{1,0:T(8,128)(2,1)S(1)}, bf16[64,512]{1,0:T(8,128)(2,1)S(1)}, u32[]{:S(2)}, u32[]{:S(2)}) collective-permute-start(bf16[64,512]{1,0:T(8,128)(2,1)S(1)} %get-tuple-element.33), channel_id=1, source_target_pairs={{0,4},{2,6},{4,0},{6,2},{8,12},{10,14},{12,8},{14,10},{1,5},{3,7},... | collective-permute-start | bytes 196616 | tf_op jit(solution)/shard_map/ppermute | solution.py:268
  13.6 2.6 %collective-permute-start.2 = (bf16[64,512]{1,0:T(8,128)(2,1)S(1)}, bf16[64,512]{1,0:T(8,128)(2,1)S(1)}, u32[]{:S(2)}, u32[]{:S(2)}) collective-permute-start(bf16[64,512]{1,0:T(8,128)(2,1)S(1)} %get-tuple-element.34), channel_id=1, source_target_pairs={{0,8},{2,10},{4,12},{6,14},{8,0},{10,2},{12,4},{14,6},{1,9},{3,11}... | collective-permute-start | bytes 196616 | tf_op jit(solution)/shard_map/ppermute | solution.py:268
  16.3 4.9 %collective-permute-done.2 = bf16[64,512]{1,0:T(8,128)(2,1)S(1)} collective-permute-done((bf16[64,512]{1,0:T(8,128)(2,1)S(1)}, bf16[64,512]{1,0:T(8,128)(2,1)S(1)}, u32[]{:S(2)}, u32[]{:S(2)}) %collective-permute-start.2) | collective-permute-done | bytes 65568 | tf_op jit(solution)/shard_map/ppermute | solution.py:268
  24.0 5.1 %collective-permute-done.4.refs_1_ = bf16[256,512]{1,0:T(8,128)(2,1)S(1)} collective-permute-done((bf16[256,512]{1,0:T(8,128)(2,1)S(1)}, bf16[256,512]{1,0:T(8,128)(2,1)S(1)}, u32[]{:S(2)}, u32[]{:S(2)}) %collective-permute-start.4) | collective-permute-done | bytes 262176 | tf_op jit(solution)/shard_map/ppermute | solution.py:268
  29.1 5.5 %patch_attention_and_ffn.3 = (bf16[64,512]{1,0:T(8,128)(2,1)S(1)}, bf16[64,512]{1,0:T(8,128)(2,1)S(1)}, bf16[64,512]{1,0:T(8,128)(2,1)S(1)}, bf16[64,512]{1,0:T(8,128)(2,1)S(1)}) custom-call(s32[3]{0:T(128)S(1)} %pad_add_fusion.place_ref, s32[2,2]{1,0:T(2,128)S(1)} %copy-done.8, bf16[256,512]{1,0:T(8,128)(2,1)S(1)} %constant_dynamic-update-slice_fusion.refs_0_, ...), custom_call_target="tpu_custom_call" | custom-call | flops 5368709120 | bytes 1048576 | tf_op jit(solution)/shard_map/patch_attention_and_ffn/pallas_call | solution.py:244
  34.7 2.7 %collective-permute-start.6 = (bf16[64,512]{1,0:T(8,128)(2,1)S(1)}, bf16[64,512]{1,0:T(8,128)(2,1)S(1)}, u32[]{:S(2)}, u32[]{:S(2)}) collective-permute-start(bf16[64,512]{1,0:T(8,128)(2,1)S(1)} %get-tuple-element.37), channel_id=1, source_target_pairs={{0,20},{2,22},{4,16},{6,18},{8,28},{10,30},{12,24},{14,26},{16,4},... | collective-permute-start | bytes 196616 | tf_op jit(solution)/shard_map/ppermute | solution.py:278
  38.3 3.2 %collective-permute-start.8 = (bf16[64,512]{1,0:T(8,128)(2,1)S(1)}, bf16[64,512]{1,0:T(8,128)(2,1)S(1)}, u32[]{:S(2)}, u32[]{:S(2)}) collective-permute-start(bf16[64,512]{1,0:T(8,128)(2,1)S(1)} %get-tuple-element.39), channel_id=1, source_target_pairs={{0,28},{2,30},{4,24},{6,26},{8,20},{10,22},{12,16},{14,18},{16,12}... | collective-permute-start | bytes 196616 | tf_op jit(solution)/shard_map/ppermute | solution.py:278
  41.5 2.7 %collective-permute-done.7 = bf16[64,512]{1,0:T(8,128)(2,1)S(1)} collective-permute-done((bf16[64,512]{1,0:T(8,128)(2,1)S(1)}, bf16[64,512]{1,0:T(8,128)(2,1)S(1)}, u32[]{:S(2)}, u32[]{:S(2)}) %collective-permute-start.7) | collective-permute-done | bytes 65568 | tf_op jit(solution)/shard_map/ppermute | solution.py:278
  46.9 3.5 %time_attention.4 = (bf16[64,512]{1,0:T(8,128)(2,1)S(1)}, bf16[64,512]{1,0:T(8,128)(2,1)S(1)}, bf16[64,512]{1,0:T(8,128)(2,1)S(1)}, bf16[64,512]{1,0:T(8,128)(2,1)S(1)}) custom-call(s32[3]{0:T(128)S(1)} %pad_add_fusion.place_ref, bf16[2,256,512]{2,1,0:T(8,128)(2,1)S(1)} %bitcast.7, bf16[2,256,512]{2,1,0:T(8,128)(2,1)S(1)} %collective-permute-done.refs_1_, ...), custom_call_target="tpu_custom_call" | custom-call | flops 5368709120 | bytes 1048576 | tf_op jit(solution)/shard_map/time_attention/pallas_call | solution.py:230
  51.3 1.6 %collective-permute-start.11 = (bf16[64,512]{1,0:T(8,128)(2,1)S(1)}, bf16[64,512]{1,0:T(8,128)(2,1)S(1)}, u32[]{:S(2)}, u32[]{:S(2)}) collective-permute-start(bf16[64,512]{1,0:T(8,128)(2,1)S(1)} %get-tuple-element.42), channel_id=1, source_target_pairs={{0,8},{2,10},{4,12},{6,14},{8,0},{10,2},{12,4},{14,6},{1,9},{3,11}... | collective-permute-start | bytes 196616 | tf_op jit(solution)/shard_map/ppermute | solution.py:268
  52.9 2.0 %collective-permute-start.12 = (bf16[64,512]{1,0:T(8,128)(2,1)S(1)}, bf16[64,512]{1,0:T(8,128)(2,1)S(1)}, u32[]{:S(2)}, u32[]{:S(2)}) collective-permute-start(bf16[64,512]{1,0:T(8,128)(2,1)S(1)} %get-tuple-element.43), channel_id=1, source_target_pairs={{0,12},{2,14},{4,8},{6,10},{8,4},{10,6},{12,0},{14,2},{1,13},{3,15... | collective-permute-start | bytes 196616 | tf_op jit(solution)/shard_map/ppermute | solution.py:268
  54.9 4.7 %collective-permute-done.11 = bf16[64,512]{1,0:T(8,128)(2,1)S(1)} collective-permute-done((bf16[64,512]{1,0:T(8,128)(2,1)S(1)}, bf16[64,512]{1,0:T(8,128)(2,1)S(1)}, u32[]{:S(2)}, u32[]{:S(2)}) %collective-permute-start.11) | collective-permute-done | bytes 65568 | tf_op jit(solution)/shard_map/ppermute | solution.py:268
  61.2 4.9 %collective-permute-done.13.refs_1_ = bf16[256,512]{1,0:T(8,128)(2,1)S(1)} collective-permute-done((bf16[256,512]{1,0:T(8,128)(2,1)S(1)}, bf16[256,512]{1,0:T(8,128)(2,1)S(1)}, u32[]{:S(2)}, u32[]{:S(2)}) %collective-permute-start.13) | collective-permute-done | bytes 262176 | tf_op jit(solution)/shard_map/ppermute | solution.py:268
  66.0 5.7 %patch_attention_and_ffn.4 = (bf16[64,512]{1,0:T(8,128)(2,1)S(1)}, bf16[64,512]{1,0:T(8,128)(2,1)S(1)}, bf16[64,512]{1,0:T(8,128)(2,1)S(1)}, bf16[64,512]{1,0:T(8,128)(2,1)S(1)}) custom-call(s32[3]{0:T(128)S(1)} %pad_add_fusion.place_ref, s32[2,2]{1,0:T(2,128)S(1)} %copy-done.8, bf16[256,512]{1,0:T(8,128)(2,1)S(1)} %constant_dynamic-update-slice_fusion.8.refs_0_, ...), custom_call_target="tpu_custom_call" | custom-call | flops 5368709120 | bytes 1048576 | tf_op jit(solution)/shard_map/patch_attention_and_ffn/pallas_call | solution.py:244
  73.1 2.2 %collective-permute-start.15 = (bf16[64,512]{1,0:T(8,128)(2,1)S(1)}, bf16[64,512]{1,0:T(8,128)(2,1)S(1)}, u32[]{:S(2)}, u32[]{:S(2)}) collective-permute-start(bf16[64,512]{1,0:T(8,128)(2,1)S(1)} %get-tuple-element.45), channel_id=1, source_target_pairs={{0,20},{2,22},{4,16},{6,18},{8,28},{10,30},{12,24},{14,26},{16,4},... | collective-permute-start | bytes 196616 | tf_op jit(solution)/shard_map/ppermute | solution.py:278
  76.5 2.0 %collective-permute-start.17 = (bf16[64,512]{1,0:T(8,128)(2,1)S(1)}, bf16[64,512]{1,0:T(8,128)(2,1)S(1)}, u32[]{:S(2)}, u32[]{:S(2)}) collective-permute-start(bf16[64,512]{1,0:T(8,128)(2,1)S(1)} %get-tuple-element.47), channel_id=1, source_target_pairs={{0,28},{2,30},{4,24},{6,26},{8,20},{10,22},{12,16},{14,18},{16,12}... | collective-permute-start | bytes 196616 | tf_op jit(solution)/shard_map/ppermute | solution.py:278
  78.6 3.3 %collective-permute-done.16 = bf16[64,512]{1,0:T(8,128)(2,1)S(1)} collective-permute-done((bf16[64,512]{1,0:T(8,128)(2,1)S(1)}, bf16[64,512]{1,0:T(8,128)(2,1)S(1)}, u32[]{:S(2)}, u32[]{:S(2)}) %collective-permute-start.16) | collective-permute-done | bytes 65568 | tf_op jit(solution)/shard_map/ppermute | solution.py:278
  81.9 1.6 %collective-permute-done.17 = bf16[64,512]{1,0:T(8,128)(2,1)S(1)} collective-permute-done((bf16[64,512]{1,0:T(8,128)(2,1)S(1)}, bf16[64,512]{1,0:T(8,128)(2,1)S(1)}, u32[]{:S(2)}, u32[]{:S(2)}) %collective-permute-start.17) | collective-permute-done | bytes 65568 | tf_op jit(solution)/shard_map/ppermute | solution.py:278
  88.2 2.0 %collective-permute-start.21 = (bf16[64,512]{1,0:T(8,128)(2,1)S(1)}, bf16[64,512]{1,0:T(8,128)(2,1)S(1)}, u32[]{:S(2)}, u32[]{:S(2)}) collective-permute-start(bf16[64,512]{1,0:T(8,128)(2,1)S(1)} %get-tuple-element.51), channel_id=1, source_target_pairs={{0,12},{2,14},{4,8},{6,10},{8,4},{10,6},{12,0},{14,2},{1,13},{3,15... | collective-permute-start | bytes 196616 | tf_op jit(solution)/shard_map/ppermute | solution.py:268
  90.2 4.7 %collective-permute-done.20 = bf16[64,512]{1,0:T(8,128)(2,1)S(1)} collective-permute-done((bf16[64,512]{1,0:T(8,128)(2,1)S(1)}, bf16[64,512]{1,0:T(8,128)(2,1)S(1)}, u32[]{:S(2)}, u32[]{:S(2)}) %collective-permute-start.20) | collective-permute-done | bytes 65568 | tf_op jit(solution)/shard_map/ppermute | solution.py:268
  94.9 1.6 %collective-permute-start.22 = (bf16[256,512]{1,0:T(8,128)(2,1)S(1)}, bf16[256,512]{1,0:T(8,128)(2,1)S(1)}, u32[]{:S(2)}, u32[]{:S(2)}) collective-permute-start(bf16[256,512]{1,0:T(8,128)(2,1)S(1)} %constant_dynamic-update-slice_fusion.16.refs_0_), channel_id=1, source_target_pairs={{0,2},{2,0},{4,6},{6,4},{8,10},{10,8},{12,14},{14,12},{1,3},{3,1},... | collective-permute-start | bytes 786440 | tf_op jit(solution)/shard_map/ppermute | solution.py:268
  96.5 5.3 %collective-permute-done.22.refs_1_ = bf16[256,512]{1,0:T(8,128)(2,1)S(1)} collective-permute-done((bf16[256,512]{1,0:T(8,128)(2,1)S(1)}, bf16[256,512]{1,0:T(8,128)(2,1)S(1)}, u32[]{:S(2)}, u32[]{:S(2)}) %collective-permute-start.22) | collective-permute-done | bytes 262176 | tf_op jit(solution)/shard_map/ppermute | solution.py:268
  102.3 8.2 %collective-permute-start.24 = (bf16[64,512]{1,0:T(8,128)(2,1)S(1)}, bf16[64,512]{1,0:T(8,128)(2,1)S(1)}, u32[]{:S(2)}, u32[]{:S(2)}) collective-permute-start(bf16[64,512]{1,0:T(8,128)(2,1)S(1)} %get-tuple-element.54), channel_id=1, source_target_pairs={{0,16},{2,18},{4,20},{6,22},{8,24},{10,26},{12,28},{14,30},{16,0},... | collective-permute-start | bytes 196616 | tf_op jit(solution)/shard_map/ppermute | solution.py:278
  110.5 1.6 %collective-permute-start.25 = (bf16[64,512]{1,0:T(8,128)(2,1)S(1)}, bf16[64,512]{1,0:T(8,128)(2,1)S(1)}, u32[]{:S(2)}, u32[]{:S(2)}) collective-permute-start(bf16[64,512]{1,0:T(8,128)(2,1)S(1)} %get-tuple-element.55), channel_id=1, source_target_pairs={{0,20},{2,22},{4,16},{6,18},{8,28},{10,30},{12,24},{14,26},{16,4},... | collective-permute-start | bytes 196616 | tf_op jit(solution)/shard_map/ppermute | solution.py:278
  112.1 1.6 %collective-permute-start.26 = (bf16[64,512]{1,0:T(8,128)(2,1)S(1)}, bf16[64,512]{1,0:T(8,128)(2,1)S(1)}, u32[]{:S(2)}, u32[]{:S(2)}) collective-permute-start(bf16[64,512]{1,0:T(8,128)(2,1)S(1)} %get-tuple-element.56), channel_id=1, source_target_pairs={{0,24},{2,26},{4,28},{6,30},{8,16},{10,18},{12,20},{14,22},{16,8},... | collective-permute-start | bytes 196616 | tf_op jit(solution)/shard_map/ppermute | solution.py:278
  113.7 2.2 %collective-permute-start.27 = (bf16[64,512]{1,0:T(8,128)(2,1)S(1)}, bf16[64,512]{1,0:T(8,128)(2,1)S(1)}, u32[]{:S(2)}, u32[]{:S(2)}) collective-permute-start(bf16[64,512]{1,0:T(8,128)(2,1)S(1)} %get-tuple-element.57), channel_id=1, source_target_pairs={{0,28},{2,30},{4,24},{6,26},{8,20},{10,22},{12,16},{14,18},{16,12}... | collective-permute-start | bytes 196616 | tf_op jit(solution)/shard_map/ppermute | solution.py:278
  117.0 1.8 %collective-permute-done.26 = bf16[64,512]{1,0:T(8,128)(2,1)S(1)} collective-permute-done((bf16[64,512]{1,0:T(8,128)(2,1)S(1)}, bf16[64,512]{1,0:T(8,128)(2,1)S(1)}, u32[]{:S(2)}, u32[]{:S(2)}) %collective-permute-start.26) | collective-permute-done | bytes 65568 | tf_op jit(solution)/shard_map/ppermute | solution.py:278
  118.9 2.0 %collective-permute-done.27 = bf16[64,512]{1,0:T(8,128)(2,1)S(1)} collective-permute-done((bf16[64,512]{1,0:T(8,128)(2,1)S(1)}, bf16[64,512]{1,0:T(8,128)(2,1)S(1)}, u32[]{:S(2)}, u32[]{:S(2)}) %collective-permute-start.27) | collective-permute-done | bytes 65568 | tf_op jit(solution)/shard_map/ppermute | solution.py:278
  121.5 5.7 %collective-permute-done.28.refs_3_ = bf16[256,512]{1,0:T(8,128)(2,1)S(1)} collective-permute-done((bf16[256,512]{1,0:T(8,128)(2,1)S(1)}, bf16[256,512]{1,0:T(8,128)(2,1)S(1)}, u32[]{:S(2)}, u32[]{:S(2)}) %collective-permute-start.28) | collective-permute-done | bytes 262176 | tf_op jit(solution)/shard_map/ppermute | solution.py:302
  127.2 1.7 %final_order.1 = bf16[2,256,512]{2,1,0:T(8,128)(2,1)} custom-call(s32[3]{0:T(128)S(1)} %pad_add_fusion.place_ref, bf16[256,512]{1,0:T(8,128)(2,1)S(1)} %constant_dynamic-update-slice_fusion.12.refs_0_, bf16[256,512]{1,0:T(8,128)(2,1)S(1)} %constant_dynamic-update-slice_fusion.20.refs_1_, bf16[256,512]{1,0:T(8,128)(2,1)S(1)} %collective-permute-done.23.refs_2_, ...), custom_call_target="tpu_custom_call" | custom-call | tf_op jit(solution)/shard_map/final_order/pallas_call | solution.py:257
  (81 shorter events, 23.7 us)
Async XLA Ops:
  0.0 2.2 %collective-permute-start = (bf16[2,256,512]{2,1,0:T(8,128)(2,1)}, bf16[2,256,512]{2,1,0:T(8,128)(2,1)S(1)}, u32[]{:S(2)}, u32[]{:S(2)}) collective-permute-start(bf16[2,256,512]{2,1,0:T(8,128)(2,1)} %bitcast.5), channel_id=1, source_target_pairs={{0,1},{1,0},{2,3},{3,2},{4,5},{5,4},{6,7},{7,6},{8,9},{9,8},{10,11... | collective-permute-start | bytes 1572872 | tf_op jit(solution)/shard_map/ppermute | solution.py:268
  7.0 22.1 %copy-start.8 = (s32[2,2]{1,0:T(2,128)S(1)}, s32[2,2]{1,0:T(2,128)}, u32[]{:S(2)}) copy-start(s32[2,2]{1,0:T(2,128)} %seen_ref.5) | copy-start | bytes 52
  7.1 22.1 %copy-start.10 = (f32[1,2,8]{2,1,0:T(2,128)S(1)}, f32[1,2,8]{2,1,0:T(2,128)}, u32[]{:S(2)}) copy-start(f32[1,2,8]{2,1,0:T(2,128)} %refs_3_.9) | copy-start | bytes 196
  10.6 5.6 %collective-permute-start.1 = (bf16[64,512]{1,0:T(8,128)(2,1)S(1)}, bf16[64,512]{1,0:T(8,128)(2,1)S(1)}, u32[]{:S(2)}, u32[]{:S(2)}) collective-permute-start(bf16[64,512]{1,0:T(8,128)(2,1)S(1)} %get-tuple-element.33), channel_id=1, source_target_pairs={{0,4},{2,6},{4,0},{6,2},{8,12},{10,14},{12,8},{14,10},{1,5},{3,7},... | collective-permute-start | bytes 196616 | tf_op jit(solution)/shard_map/ppermute | solution.py:268
  13.6 7.5 %collective-permute-start.2 = (bf16[64,512]{1,0:T(8,128)(2,1)S(1)}, bf16[64,512]{1,0:T(8,128)(2,1)S(1)}, u32[]{:S(2)}, u32[]{:S(2)}) collective-permute-start(bf16[64,512]{1,0:T(8,128)(2,1)S(1)} %get-tuple-element.34), channel_id=1, source_target_pairs={{0,8},{2,10},{4,12},{6,14},{8,0},{10,2},{12,4},{14,6},{1,9},{3,11}... | collective-permute-start | bytes 196616 | tf_op jit(solution)/shard_map/ppermute | solution.py:268
  16.2 6.2 %collective-permute-start.3 = (bf16[64,512]{1,0:T(8,128)(2,1)S(1)}, bf16[64,512]{1,0:T(8,128)(2,1)S(1)}, u32[]{:S(2)}, u32[]{:S(2)}) collective-permute-start(bf16[64,512]{1,0:T(8,128)(2,1)S(1)} %get-tuple-element.35), channel_id=1, source_target_pairs={{0,12},{2,14},{4,8},{6,10},{8,4},{10,6},{12,0},{14,2},{1,13},{3,15... | collective-permute-start | bytes 196616 | tf_op jit(solution)/shard_map/ppermute | solution.py:268
  22.4 24.5 %copy-start.7 = (bf16[2,16,16,512]{3,2,1,0:T(8,128)(2,1)S(1)}, bf16[2,16,16,512]{3,2,1,0:T(8,128)(2,1)}, u32[]{:S(2)}) copy-start(bf16[2,16,16,512]{3,2,1,0:T(8,128)(2,1)} %param.8) | copy-start | bytes 1572868
  22.4 6.7 %collective-permute-start.4 = (bf16[256,512]{1,0:T(8,128)(2,1)S(1)}, bf16[256,512]{1,0:T(8,128)(2,1)S(1)}, u32[]{:S(2)}, u32[]{:S(2)}) collective-permute-start(bf16[256,512]{1,0:T(8,128)(2,1)S(1)} %constant_dynamic-update-slice_fusion.refs_0_), channel_id=1, source_target_pairs={{0,2},{2,0},{4,6},{6,4},{8,10},{10,8},{12,14},{14,12},{1,3},{3,1},... | collective-permute-start | bytes 786440 | tf_op jit(solution)/shard_map/ppermute | solution.py:268
  34.7 6.8 %collective-permute-start.5 = (bf16[64,512]{1,0:T(8,128)(2,1)S(1)}, bf16[64,512]{1,0:T(8,128)(2,1)S(1)}, u32[]{:S(2)}, u32[]{:S(2)}) collective-permute-start(bf16[64,512]{1,0:T(8,128)(2,1)S(1)} %get-tuple-element.36), channel_id=1, source_target_pairs={{0,16},{2,18},{4,20},{6,22},{8,24},{10,26},{12,28},{14,30},{16,0},... | collective-permute-start | bytes 196616 | tf_op jit(solution)/shard_map/ppermute | solution.py:278
  34.7 6.8 %collective-permute-start.6 = (bf16[64,512]{1,0:T(8,128)(2,1)S(1)}, bf16[64,512]{1,0:T(8,128)(2,1)S(1)}, u32[]{:S(2)}, u32[]{:S(2)}) collective-permute-start(bf16[64,512]{1,0:T(8,128)(2,1)S(1)} %get-tuple-element.37), channel_id=1, source_target_pairs={{0,20},{2,22},{4,16},{6,18},{8,28},{10,30},{12,24},{14,26},{16,4},... | collective-permute-start | bytes 196616 | tf_op jit(solution)/shard_map/ppermute | solution.py:278
  37.4 6.8 %collective-permute-start.7 = (bf16[64,512]{1,0:T(8,128)(2,1)S(1)}, bf16[64,512]{1,0:T(8,128)(2,1)S(1)}, u32[]{:S(2)}, u32[]{:S(2)}) collective-permute-start(bf16[64,512]{1,0:T(8,128)(2,1)S(1)} %get-tuple-element.38), channel_id=1, source_target_pairs={{0,24},{2,26},{4,28},{6,30},{8,16},{10,18},{12,20},{14,22},{16,8},... | collective-permute-start | bytes 196616 | tf_op jit(solution)/shard_map/ppermute | solution.py:278
  38.3 7.1 %collective-permute-start.8 = (bf16[64,512]{1,0:T(8,128)(2,1)S(1)}, bf16[64,512]{1,0:T(8,128)(2,1)S(1)}, u32[]{:S(2)}, u32[]{:S(2)}) collective-permute-start(bf16[64,512]{1,0:T(8,128)(2,1)S(1)} %get-tuple-element.39), channel_id=1, source_target_pairs={{0,28},{2,30},{4,24},{6,26},{8,20},{10,22},{12,16},{14,18},{16,12}... | collective-permute-start | bytes 196616 | tf_op jit(solution)/shard_map/ppermute | solution.py:278
  45.3 1.5 %collective-permute-start.9 = (bf16[256,512]{1,0:T(8,128)(2,1)S(1)}, bf16[256,512]{1,0:T(8,128)(2,1)S(1)}, u32[]{:S(2)}, u32[]{:S(2)}) collective-permute-start(bf16[256,512]{1,0:T(8,128)(2,1)S(1)} %constant_dynamic-update-slice_fusion.4.refs_2_), channel_id=1, source_target_pairs={{0,1},{1,0},{2,3},{3,2},{4,5},{5,4},{6,7},{7,6},{8,9},{9,8},{10,11... | collective-permute-start | bytes 786440 | tf_op jit(solution)/shard_map/ppermute | solution.py:268
  50.4 4.5 %collective-permute-start.10 = (bf16[64,512]{1,0:T(8,128)(2,1)S(1)}, bf16[64,512]{1,0:T(8,128)(2,1)S(1)}, u32[]{:S(2)}, u32[]{:S(2)}) collective-permute-start(bf16[64,512]{1,0:T(8,128)(2,1)S(1)} %get-tuple-element.41), channel_id=1, source_target_pairs={{0,4},{2,6},{4,0},{6,2},{8,12},{10,14},{12,8},{14,10},{1,5},{3,7},... | collective-permute-start | bytes 196616 | tf_op jit(solution)/shard_map/ppermute | solution.py:268
  51.3 8.3 %collective-permute-start.11 = (bf16[64,512]{1,0:T(8,128)(2,1)S(1)}, bf16[64,512]{1,0:T(8,128)(2,1)S(1)}, u32[]{:S(2)}, u32[]{:S(2)}) collective-permute-start(bf16[64,512]{1,0:T(8,128)(2,1)S(1)} %get-tuple-element.42), channel_id=1, source_target_pairs={{0,8},{2,10},{4,12},{6,14},{8,0},{10,2},{12,4},{14,6},{1,9},{3,11}... | collective-permute-start | bytes 196616 | tf_op jit(solution)/shard_map/ppermute | solution.py:268
  52.9 6.7 %collective-permute-start.12 = (bf16[64,512]{1,0:T(8,128)(2,1)S(1)}, bf16[64,512]{1,0:T(8,128)(2,1)S(1)}, u32[]{:S(2)}, u32[]{:S(2)}) collective-permute-start(bf16[64,512]{1,0:T(8,128)(2,1)S(1)} %get-tuple-element.43), channel_id=1, source_target_pairs={{0,12},{2,14},{4,8},{6,10},{8,4},{10,6},{12,0},{14,2},{1,13},{3,15... | collective-permute-start | bytes 196616 | tf_op jit(solution)/shard_map/ppermute | solution.py:268
  59.6 6.4 %collective-permute-start.13 = (bf16[256,512]{1,0:T(8,128)(2,1)S(1)}, bf16[256,512]{1,0:T(8,128)(2,1)S(1)}, u32[]{:S(2)}, u32[]{:S(2)}) collective-permute-start(bf16[256,512]{1,0:T(8,128)(2,1)S(1)} %constant_dynamic-update-slice_fusion.8.refs_0_), channel_id=1, source_target_pairs={{0,2},{2,0},{4,6},{6,4},{8,10},{10,8},{12,14},{14,12},{1,3},{3,1},... | collective-permute-start | bytes 786440 | tf_op jit(solution)/shard_map/ppermute | solution.py:268
  71.8 6.8 %collective-permute-start.14 = (bf16[64,512]{1,0:T(8,128)(2,1)S(1)}, bf16[64,512]{1,0:T(8,128)(2,1)S(1)}, u32[]{:S(2)}, u32[]{:S(2)}) collective-permute-start(bf16[64,512]{1,0:T(8,128)(2,1)S(1)} %get-tuple-element.44), channel_id=1, source_target_pairs={{0,16},{2,18},{4,20},{6,22},{8,24},{10,26},{12,28},{14,30},{16,0},... | collective-permute-start | bytes 196616 | tf_op jit(solution)/shard_map/ppermute | solution.py:278
  73.1 5.5 %collective-permute-start.15 = (bf16[64,512]{1,0:T(8,128)(2,1)S(1)}, bf16[64,512]{1,0:T(8,128)(2,1)S(1)}, u32[]{:S(2)}, u32[]{:S(2)}) collective-permute-start(bf16[64,512]{1,0:T(8,128)(2,1)S(1)} %get-tuple-element.45), channel_id=1, source_target_pairs={{0,20},{2,22},{4,16},{6,18},{8,28},{10,30},{12,24},{14,26},{16,4},... | collective-permute-start | bytes 196616 | tf_op jit(solution)/shard_map/ppermute | solution.py:278
  75.3 6.7 %collective-permute-start.16 = (bf16[64,512]{1,0:T(8,128)(2,1)S(1)}, bf16[64,512]{1,0:T(8,128)(2,1)S(1)}, u32[]{:S(2)}, u32[]{:S(2)}) collective-permute-start(bf16[64,512]{1,0:T(8,128)(2,1)S(1)} %get-tuple-element.46), channel_id=1, source_target_pairs={{0,24},{2,26},{4,28},{6,30},{8,16},{10,18},{12,20},{14,22},{16,8},... | collective-permute-start | bytes 196616 | tf_op jit(solution)/shard_map/ppermute | solution.py:278
  76.5 7.1 %collective-permute-start.17 = (bf16[64,512]{1,0:T(8,128)(2,1)S(1)}, bf16[64,512]{1,0:T(8,128)(2,1)S(1)}, u32[]{:S(2)}, u32[]{:S(2)}) collective-permute-start(bf16[64,512]{1,0:T(8,128)(2,1)S(1)} %get-tuple-element.47), channel_id=1, source_target_pairs={{0,28},{2,30},{4,24},{6,26},{8,20},{10,22},{12,16},{14,18},{16,12}... | collective-permute-start | bytes 196616 | tf_op jit(solution)/shard_map/ppermute | solution.py:278
  83.6 1.5 %collective-permute-start.18 = (bf16[256,512]{1,0:T(8,128)(2,1)S(1)}, bf16[256,512]{1,0:T(8,128)(2,1)S(1)}, u32[]{:S(2)}, u32[]{:S(2)}) collective-permute-start(bf16[256,512]{1,0:T(8,128)(2,1)S(1)} %constant_dynamic-update-slice_fusion.12.refs_0_), channel_id=1, source_target_pairs={{0,1},{1,0},{2,3},{3,2},{4,5},{5,4},{6,7},{7,6},{8,9},{9,8},{10,11... | collective-permute-start | bytes 786440 | tf_op jit(solution)/shard_map/ppermute | solution.py:268
  83.6 12.9 %collective-permute-start.23 = (bf16[256,512]{1,0:T(8,128)(2,1)S(1)}, bf16[256,512]{1,0:T(8,128)(2,1)S(1)}, u32[]{:S(2)}, u32[]{:S(2)}) collective-permute-start(bf16[256,512]{1,0:T(8,128)(2,1)S(1)} %constant_dynamic-update-slice_fusion.12.refs_0_), channel_id=1, source_target_pairs={{0,16},{16,0},{1,17},{17,1},{2,18},{18,2},{3,19},{19,3},{4,20},{20... | collective-permute-start | bytes 786440 | tf_op jit(solution)/shard_map/ppermute | solution.py:302
  85.7 4.5 %collective-permute-start.19 = (bf16[64,512]{1,0:T(8,128)(2,1)S(1)}, bf16[64,512]{1,0:T(8,128)(2,1)S(1)}, u32[]{:S(2)}, u32[]{:S(2)}) collective-permute-start(bf16[64,512]{1,0:T(8,128)(2,1)S(1)} %get-tuple-element.49), channel_id=1, source_target_pairs={{0,4},{2,6},{4,0},{6,2},{8,12},{10,14},{12,8},{14,10},{1,5},{3,7},... | collective-permute-start | bytes 196616 | tf_op jit(solution)/shard_map/ppermute | solution.py:268
  86.9 8.0 %collective-permute-start.20 = (bf16[64,512]{1,0:T(8,128)(2,1)S(1)}, bf16[64,512]{1,0:T(8,128)(2,1)S(1)}, u32[]{:S(2)}, u32[]{:S(2)}) collective-permute-start(bf16[64,512]{1,0:T(8,128)(2,1)S(1)} %get-tuple-element.50), channel_id=1, source_target_pairs={{0,8},{2,10},{4,12},{6,14},{8,0},{10,2},{12,4},{14,6},{1,9},{3,11}... | collective-permute-start | bytes 196616 | tf_op jit(solution)/shard_map/ppermute | solution.py:268
  88.2 6.7 %collective-permute-start.21 = (bf16[64,512]{1,0:T(8,128)(2,1)S(1)}, bf16[64,512]{1,0:T(8,128)(2,1)S(1)}, u32[]{:S(2)}, u32[]{:S(2)}) collective-permute-start(bf16[64,512]{1,0:T(8,128)(2,1)S(1)} %get-tuple-element.51), channel_id=1, source_target_pairs={{0,12},{2,14},{4,8},{6,10},{8,4},{10,6},{12,0},{14,2},{1,13},{3,15... | collective-permute-start | bytes 196616 | tf_op jit(solution)/shard_map/ppermute | solution.py:268
  94.9 6.8 %collective-permute-start.22 = (bf16[256,512]{1,0:T(8,128)(2,1)S(1)}, bf16[256,512]{1,0:T(8,128)(2,1)S(1)}, u32[]{:S(2)}, u32[]{:S(2)}) collective-permute-start(bf16[256,512]{1,0:T(8,128)(2,1)S(1)} %constant_dynamic-update-slice_fusion.16.refs_0_), channel_id=1, source_target_pairs={{0,2},{2,0},{4,6},{6,4},{8,10},{10,8},{12,14},{14,12},{1,3},{3,1},... | collective-permute-start | bytes 786440 | tf_op jit(solution)/shard_map/ppermute | solution.py:268
  102.3 13.6 %collective-permute-start.24 = (bf16[64,512]{1,0:T(8,128)(2,1)S(1)}, bf16[64,512]{1,0:T(8,128)(2,1)S(1)}, u32[]{:S(2)}, u32[]{:S(2)}) collective-permute-start(bf16[64,512]{1,0:T(8,128)(2,1)S(1)} %get-tuple-element.54), channel_id=1, source_target_pairs={{0,16},{2,18},{4,20},{6,22},{8,24},{10,26},{12,28},{14,30},{16,0},... | collective-permute-start | bytes 196616 | tf_op jit(solution)/shard_map/ppermute | solution.py:278
  110.5 6.5 %collective-permute-start.25 = (bf16[64,512]{1,0:T(8,128)(2,1)S(1)}, bf16[64,512]{1,0:T(8,128)(2,1)S(1)}, u32[]{:S(2)}, u32[]{:S(2)}) collective-permute-start(bf16[64,512]{1,0:T(8,128)(2,1)S(1)} %get-tuple-element.55), channel_id=1, source_target_pairs={{0,20},{2,22},{4,16},{6,18},{8,28},{10,30},{12,24},{14,26},{16,4},... | collective-permute-start | bytes 196616 | tf_op jit(solution)/shard_map/ppermute | solution.py:278
  112.1 6.7 %collective-permute-start.26 = (bf16[64,512]{1,0:T(8,128)(2,1)S(1)}, bf16[64,512]{1,0:T(8,128)(2,1)S(1)}, u32[]{:S(2)}, u32[]{:S(2)}) collective-permute-start(bf16[64,512]{1,0:T(8,128)(2,1)S(1)} %get-tuple-element.56), channel_id=1, source_target_pairs={{0,24},{2,26},{4,28},{6,30},{8,16},{10,18},{12,20},{14,22},{16,8},... | collective-permute-start | bytes 196616 | tf_op jit(solution)/shard_map/ppermute | solution.py:278
  113.7 7.1 %collective-permute-start.27 = (bf16[64,512]{1,0:T(8,128)(2,1)S(1)}, bf16[64,512]{1,0:T(8,128)(2,1)S(1)}, u32[]{:S(2)}, u32[]{:S(2)}) collective-permute-start(bf16[64,512]{1,0:T(8,128)(2,1)S(1)} %get-tuple-element.57), channel_id=1, source_target_pairs={{0,28},{2,30},{4,24},{6,26},{8,20},{10,22},{12,16},{14,18},{16,12}... | collective-permute-start | bytes 196616 | tf_op jit(solution)/shard_map/ppermute | solution.py:278
  120.9 6.4 %collective-permute-start.28 = (bf16[256,512]{1,0:T(8,128)(2,1)S(1)}, bf16[256,512]{1,0:T(8,128)(2,1)S(1)}, u32[]{:S(2)}, u32[]{:S(2)}) collective-permute-start(bf16[256,512]{1,0:T(8,128)(2,1)S(1)} %constant_dynamic-update-slice_fusion.20.refs_1_), channel_id=1, source_target_pairs={{0,16},{16,0},{1,17},{17,1},{2,18},{18,2},{3,19},{19,3},{4,20},{20... | collective-permute-start | bytes 786440 | tf_op jit(solution)/shard_map/ppermute | solution.py:302
  (8 other events, 93.1 us)
where the time goes:
time: 129 us
  waiting for transfers between devices  53.3 us (41%)
  starting transfers between devices  48.4 us (38%)
  Pallas kernels  21.1 us (16%)
  local copies, waits for them, and re-layouts  5.69 us (4%)
    ppermute x15, waiting for transfers between devices, flipped(): lax.ppermute(x, axis, [(s, s ^ k) for s in range(lax.axis_size(axis))])  33.9 us
    ppermute x12, starting transfers between devices, handed_on(): return lax.ppermute(x, ('pipe', 'patch'), pairs)  27.2 us
    ppermute x15, starting transfers between devices, flipped(): lax.ppermute(x, axis, [(s, s ^ k) for s in range(lax.axis_size(axis))])  19.6 us
    ppermute x12, waiting for transfers between devices, handed_on(): return lax.ppermute(x, ('pipe', 'patch'), pairs)  13.7 us
    pallas_call x3, Pallas kernels, call_patch(): pl.pallas_call(functools.partial(patch_kernel, sizes, step, micro), out_s...  11.8 us
    pallas_call x3, Pallas kernels, call_time(): pl.pallas_call(functools.partial(time_kernel, sizes, step, micro), out_sh...  7.66 us
    ppermute x2, waiting for transfers between devices, onward(): return lax.ppermute(x, 'pipe', [(s, (s + 1) % pipes) for s in range(pipes)])  5.72 us
    unnamed x41, local copies, waits for them, and re-layouts  5.66 us
  transfers between devices with their start and end apart: 29, of which 18 were waited for; matrix products, arithmetic and copies ran while one was open for 1% of the time, Pallas kernels for 0%

commit v1 on v0

--- a/solution.py
+++ b/solution.py
@@ -95,7 +95,7 @@
 def time_kernel(sizes, step, micro, place_ref, *refs):
     shards, peers, patches, hl = sizes
     given = peers if step < micro else 0
-    came = peers if step > 0 else 0
+    came = peers * shards if step > 0 else 0
     input_refs, refs = refs[:given], refs[given:]
     came_refs, refs = refs[:came], refs[came:]
     (gain_ref, scale_ref, w_in_ref, w_out_ref), refs = refs[:4], refs[4:]
@@ -122,7 +122,8 @@
             @pl.when(place_ref[0] != 0)
             def _():
                 for j, ref in enumerate(came_refs):
-                    x_ref[j * rows : (j + 1) * rows, :] = ref[...]
+                    size = rows // shards
+                    x_ref[j * size : (j + 1) * size, :] = ref[...]
 
         x = x_ref[...].astype(jnp.float32)
         mine = digits((rows, rows * peers), 0, hl, patches)[1]
@@ -143,18 +144,22 @@
             y_refs[k][...] = y[k * size : (k + 1) * size]
 
 
-def patch_kernel(sizes, step, micro, place_ref, seen_ref, *refs):
+def patch_kernel(sizes, step, micro, outs, place_ref, seen_ref, *refs):
     slow, _, patches, hl = sizes
-    fast = len(refs) - 6 - slow
+    count = len(refs) - 6 - outs
+    fast = count // slow
     x_refs, (gain_ref, scale_ref, w_in_ref, w_out_ref, up_ref, down_ref), y_refs = (
-        refs[:fast],
-        refs[fast : fast + 6],
-        refs[fast + 6 :],
+        refs[:count],
+        refs[count : count + 6],
+        refs[count + 6 :],
     )
 
     @pl.when(at_work(place_ref, step, micro))
     def _():
-        xs = [x_ref[...].astype(jnp.float32) for x_ref in x_refs]
+        xs = [
+            jnp.concatenate([ref[...] for ref in x_refs[i : i + slow]], axis=0).astype(jnp.float32)
+            for i in range(0, count, slow)
+        ]
         x = xs[0]
         rows = x.shape[0]
         shape = (rows, rows * fast)
@@ -193,25 +198,41 @@
             hidden = (0.5 * u * (1.0 + bent)).astype(jnp.bfloat16)
             total = total + matmul(hidden, down_ref[0, start : start + chunk, :])
         y = total.astype(jnp.bfloat16)
-        size = rows // slow
-        for k in range(slow):
+        size = rows // outs
+        for k in range(outs):
             y_refs[k][...] = y[k * size : (k + 1) * size]
 
 
-def final_kernel(sizes, micro, place_ref, *refs):
-    shards, _, patches, hl = sizes
+def pick_kernel(slow, last, place_ref, *refs):
+    x_refs, y_refs = refs[:-slow], refs[-slow:]
+    size = x_refs[0].shape[0] // slow
+    for hops, x_ref in enumerate(x_refs):
+
+        @pl.when(place_ref[0] == (last + hops) % len(x_refs))
+        def _():
+            for k, y_ref in enumerate(y_refs):
+                y_ref[...] = x_ref[k * size : (k + 1) * size, :]
+
+
+def final_kernel(sizes, early, place_ref, *refs):
+    slow, _, patches, hl = sizes
     y_ref = refs[-1]
-    rows = shards * patches * hl
-    late, shard, patch = digits((rows, rows), 0, hl, shards)
+    block_refs = refs[-1 - slow : -1]
+    rows = slow * patches * hl
+    late, shard, patch = digits((rows, rows), 0, hl, slow)
     source = lax.broadcasted_iota(jnp.int32, (rows, rows), 1)
     wanted = ((shard ^ place_ref[1]) * patches + patch) * hl + late
     order = jnp.where(wanted == source, 1.0, 0.0).astype(jnp.bfloat16)
-    for hops in range(len(refs) // micro):
-
-        @pl.when(place_ref[0] == hops)
-        def _():
-            for m in range(micro):
-                y_ref[m] = matmul(order, refs[hops * micro + m][...]).astype(jnp.bfloat16)
+    if early:
+        for stage in range((len(refs) - 1 - slow) // early):
+
+            @pl.when(place_ref[0] == stage)
+            def _():
+                for m in range(early):
+                    y_ref[m] = matmul(order, refs[stage * early + m][...]).astype(jnp.bfloat16)
+
+    x = jnp.concatenate([ref[...] for ref in block_refs], axis=0)
+    y_ref[early] = matmul(order, x).astype(jnp.bfloat16)
 
 
 VMEM = pl.BlockSpec(memory_space=pltpu.VMEM)
@@ -225,7 +246,7 @@
 
 
 def call_time(sizes, step, micro, place, given, came, gains, scales, w_in, w_out):
-    rows, width = given[0].shape[1:] if given else came[0].shape
+    rows, width = given[0].shape[1:] if given else (sizes[0] * came[0].shape[0], came[0].shape[1])
     xs = list(given) + list(came)
     return pl.pallas_call(
         functools.partial(time_kernel, sizes, step, micro),
@@ -239,23 +260,35 @@
     )(place, *xs, gains, scales, w_in, w_out)
 
 
-def call_patch(sizes, step, micro, place, seen, xs, gains, scales, w_in, w_out, w_up, w_down):
-    rows, width = xs[0].shape
+def call_patch(sizes, step, micro, outs, place, seen, xs, gains, scales, w_in, w_out, w_up, w_down):
+    rows, width = sizes[0] * xs[0].shape[0], xs[0].shape[1]
     return pl.pallas_call(
-        functools.partial(patch_kernel, sizes, step, micro),
-        out_shape=blocks_of(sizes[0], rows, width),
+        functools.partial(patch_kernel, sizes, step, micro, outs),
+        out_shape=blocks_of(outs, rows, width),
         in_specs=[SMEM, SMEM] + [VMEM] * len(xs) + [VMEM, SMEM] + [VMEM] * 4,
-        out_specs=[VMEM] * sizes[0],
+        out_specs=[VMEM] * outs,
         compiler_params=PARAMS,
         cost_estimate=COST,
         name="patch_attention_and_ffn",
     )(place, seen, *xs, gains, scales, w_in, w_out, w_up, w_down)
 
 
+def call_pick(slow, last, place, xs):
+    rows, width = xs[0].shape
+    return pl.pallas_call(
+        functools.partial(pick_kernel, slow, last),
+        out_shape=blocks_of(slow, rows, width),
+        in_specs=[SMEM] + [VMEM] * len(xs),
+        out_specs=[VMEM] * slow,
+        compiler_params=PARAMS,
+        name="pick",
+    )(place, *xs)
+
+
 def call_final(sizes, place, shape, parts):
     micro, rows, width = shape
     return pl.pallas_call(
-        functools.partial(final_kernel, sizes, micro),
+        functools.partial(final_kernel, sizes, micro - 1),
         out_shape=jax.ShapeDtypeStruct((micro, rows, width), jnp.bfloat16),
         in_specs=[SMEM] + [VMEM] * len(parts),
         out_specs=VMEM,
@@ -287,45 +320,60 @@
     fast = 2
     slow = shards // fast
     sizes = (slow, peers, patches, hours // slow)
+    last = pipes - 1
     shard = lax.axis_index("patch")
     place = jnp.stack([lax.axis_index("pipe"), lax.div(shard, fast), lax.rem(shard, fast)])
     order = sorted(range(slow), key=lambda k: (k < slow // 2, k))
 
-    def with_others(x, axis, count):
-        return [x] + [flipped(x, axis, j) for j in range(1, count)]
+    def gathered(blocks, axis, count):
+        out = list(blocks)
+        for j in range(1, count):
+            got = {k: flipped(blocks[k], axis, j) for k in reversed(order)}
+            out += [got[k] for k in range(len(blocks))]
+        return out
 
     def along_slow(blocks, send, first):
         got = {k: send(blocks[k], k * fast) for k in order if k >= first}
-        return jnp.concatenate([got.get(k, blocks[k]) for k in range(slow)])
+        return [got.get(k, blocks[k]) for k in range(slow)]
+
+    def in_stage(x, k):
+        return flipped(x, "patch", k)
 
     def onward(x):
         return lax.ppermute(x, "pipe", [(s, (s + 1) % pipes) for s in range(pipes)])
 
-    given = with_others(inputs.reshape(micro, rows, width), "hour", peers)
+    x = inputs.reshape(micro, rows, width)
+    given = [x] + [flipped(x, "hour", j) for j in range(1, peers)]
     came = []
-    finished = []
+    early = []
     back = []
     for step in range(micro + pipes - 1):
-        if step > 0:
-            came = with_others(arrived, "hour", peers)
         now = given if step < micro else []
         mixed = call_time(sizes, step, micro, place, now, came, gains, scales, w_in, w_out)
-        own = along_slow(mixed, lambda x, k: flipped(x, "patch", k), 1)
-        spread = with_others(own, "patch", fast)
+        own = along_slow(mixed, in_stage, 1)
+        spread = gathered(own, "patch", fast)
         if back:
             spread, back = lax.optimization_barrier((spread, back))
-            finished[-1][1:] = back
+            early.append(back)
+        at_end = step == micro + pipes - 2
+        outs = 1 if at_end else slow
         done = call_patch(
-            sizes, step, micro, place, seen, spread, gains, scales, w_in, w_out, w_up, w_down
+            sizes, step, micro, outs, place, seen, spread, gains, scales, w_in, w_out, w_up, w_down
         )
-        arrived = along_slow(done, handed_on, 0)
-        back = []
-        if step >= pipes - 1:
-            for _ in range(1, pipes):
-                back.append(onward(back[-1] if back else arrived))
-            finished.append([arrived] + back)
-    parts = [copies[hops] for hops in range(pipes) for copies in finished]
-    return call_final(sizes, place, (micro, rows, width), parts).reshape(inputs.shape)
+        if not at_end:
+            arrived = along_slow(done, handed_on, 0)
+            came = gathered(arrived, "hour", peers)
+            if step >= last:
+                back = [jnp.concatenate(arrived)]
+                for _ in range(1, pipes):
+                    back.append(onward(back[-1]))
+    done = list(done)
+    for _ in range(1, pipes):
+        done.append(onward(done[-1]))
+    blocks = along_slow(call_pick(slow, last, place, done), in_stage, 1)
+    parts = [copies[stage] for stage in range(pipes) for copies in early] if early else []
+    out = call_final(sizes, place, (micro, rows, width), parts + blocks)
+    return out.reshape(inputs.shape)
 
 
 def solution(mesh):

time: 129 us -> 122 us (0.946)
  waiting for transfers between devices: 53.3 us -> 37.4 us
  starting transfers between devices: 48.4 us -> 56.2 us
    ppermute x15 -> x33, starting transfers between devices: 19.6 us -> 33.6 us  [flipped(): lax.ppermute(x, axis, [(s, s ^ k) for s in range(lax.axis_size(axis))])]
    ppermute x12 -> x8, starting transfers between devices: 27.2 us -> 13.6 us  [handed_on(): return lax.ppermute(x, ('pipe', 'patch'), pairs)]
    ppermute x15 -> x33, waiting for transfers between devices: 33.9 us -> 24.3 us  [flipped(): lax.ppermute(x, axis, [(s, s ^ k) for s in range(lax.axis_size(axis))])]
    ppermute x2, starting transfers between devices: 1.59 us -> 9.04 us  [onward(): return lax.ppermute(x, 'pipe', [(s, (s + 1) % pipes) for s in range(pipes)])]
    ppermute x12 -> x8, waiting for transfers between devices: 13.7 us -> 8.58 us  [handed_on(): return lax.ppermute(x, ('pipe', 'patch'), pairs)]
    pallas_call x4 -> x5, Pallas kernels: 13.5 us -> 14.2 us  [the longest x3 11.8 us: call_patch(): pl.pallas_call(functools.partial(patch_kernel, sizes, step, micro, outs),...]
    unnamed x41 -> x26, local copies, waits for them, and re-layouts: 5.66 us -> 5.57 us
  transfers between devices with their start and end apart: 29 -> 43, of which waited for: 18 -> 24; matrix products, arithmetic and copies ran while one was open for 1% -> 1% of each run, Pallas kernels for 0% -> 0%
where the time goes in v1:
time: 122 us; the launch traced here: 121 us
  starting transfers between devices  56.2 us (46%)
  waiting for transfers between devices  37.4 us (31%)
  Pallas kernels  21.9 us (18%)
  local copies, waits for them, and re-layouts  5.58 us (5%)
    ppermute x33, starting transfers between devices, flipped(): lax.ppermute(x, axis, [(s, s ^ k) for s in range(lax.axis_size(axis))])  33.6 us
    ppermute x33, waiting for transfers between devices, flipped(): lax.ppermute(x, axis, [(s, s ^ k) for s in range(lax.axis_size(axis))])  24.3 us
    ppermute x8, starting transfers between devices, handed_on(): return lax.ppermute(x, ('pipe', 'patch'), pairs)  13.6 us
    pallas_call x3, Pallas kernels, call_patch(): pl.pallas_call(functools.partial(patch_kernel, sizes, step, micro, outs),...  11.8 us
    ppermute x2, starting transfers between devices, onward(): return lax.ppermute(x, 'pipe', [(s, (s + 1) % pipes) for s in range(pipes)])  9.04 us
    ppermute x8, waiting for transfers between devices, handed_on(): return lax.ppermute(x, ('pipe', 'patch'), pairs)  8.58 us
    pallas_call x3, Pallas kernels, call_time(): pl.pallas_call(functools.partial(time_kernel, sizes, step, micro), out_sh...  7.66 us
    unnamed x26, local copies, waits for them, and re-layouts  5.57 us
  transfers between devices with their start and end apart: 43, of which 24 were waited for; matrix products, arithmetic and copies ran while one was open for 1% of the time, Pallas kernels for 0%

profile of v1, /device:TPU:0, one launch (start us, length us, event | category | flops | bytes accessed | tf_op | source)
XLA Modules:
  0.0 121.3 jit_solution(2326091143168833432)
XLA Ops:
  2.2 1.9 %copy-done = bf16[1,2,512,1536]{3,2,1,0:T(8,128)(2,1)S(1)} copy-done((bf16[1,2,512,1536]{3,2,1,0:T(8,128)(2,1)S(1)}, bf16[1,2,512,1536]{3,2,1,0:T(8,128)(2,1)}, u32[]{:S(2)}) %copy-start) | copy-done | bytes 3145752
  7.1 3.6 %time_attention.3 = (bf16[64,512]{1,0:T(8,128)(2,1)S(1)}, bf16[64,512]{1,0:T(8,128)(2,1)S(1)}, bf16[64,512]{1,0:T(8,128)(2,1)S(1)}, bf16[64,512]{1,0:T(8,128)(2,1)S(1)}) custom-call(s32[3]{0:T(128)S(1)} %pad_add_fusion.place_ref, bf16[2,256,512]{2,1,0:T(8,128)(2,1)S(1)} %bitcast.6, bf16[2,256,512]{2,1,0:T(8,128)(2,1)S(1)} %collective-permute-done.refs_1_, ...), custom_call_target="tpu_custom_call" | custom-call | flops 5368709120 | bytes 1048576 | tf_op jit(solution)/shard_map/time_attention/pallas_call | solution.py:251
  10.6 3.0 %collective-permute-start.1 = (bf16[64,512]{1,0:T(8,128)(2,1)S(1)}, bf16[64,512]{1,0:T(8,128)(2,1)S(1)}, u32[]{:S(2)}, u32[]{:S(2)}) collective-permute-start(bf16[64,512]{1,0:T(8,128)(2,1)S(1)} %get-tuple-element.40), channel_id=1, source_target_pairs={{0,4},{2,6},{4,0},{6,2},{8,12},{10,14},{12,8},{14,10},{1,5},{3,7},... | collective-permute-start | bytes 196616 | tf_op jit(solution)/shard_map/ppermute | solution.py:301
  13.6 2.6 %collective-permute-start.2 = (bf16[64,512]{1,0:T(8,128)(2,1)S(1)}, bf16[64,512]{1,0:T(8,128)(2,1)S(1)}, u32[]{:S(2)}, u32[]{:S(2)}) collective-permute-start(bf16[64,512]{1,0:T(8,128)(2,1)S(1)} %get-tuple-element.41), channel_id=1, source_target_pairs={{0,8},{2,10},{4,12},{6,14},{8,0},{10,2},{12,4},{14,6},{1,9},{3,11}... | collective-permute-start | bytes 196616 | tf_op jit(solution)/shard_map/ppermute | solution.py:301
  16.2 1.7 %collective-permute-start.4 = (bf16[64,512]{1,0:T(8,128)(2,1)S(1)}, bf16[64,512]{1,0:T(8,128)(2,1)S(1)}, u32[]{:S(2)}, u32[]{:S(2)}) collective-permute-start(bf16[64,512]{1,0:T(8,128)(2,1)S(1)} %get-tuple-element.39.refs_0_), channel_id=1, source_target_pairs={{0,2},{2,0},{4,6},{6,4},{8,10},{10,8},{12,14},{14,12},{1,3},{3,1},... | collective-permute-start | bytes 196616 | tf_op jit(solution)/shard_map/ppermute | solution.py:301
  18.3 2.9 %collective-permute-done.2.refs_2_ = bf16[64,512]{1,0:T(8,128)(2,1)S(1)} collective-permute-done((bf16[64,512]{1,0:T(8,128)(2,1)S(1)}, bf16[64,512]{1,0:T(8,128)(2,1)S(1)}, u32[]{:S(2)}, u32[]{:S(2)}) %collective-permute-start.2) | collective-permute-done | bytes 65568 | tf_op jit(solution)/shard_map/ppermute | solution.py:301
  23.9 1.5 %collective-permute-done.6.refs_6_ = bf16[64,512]{1,0:T(8,128)(2,1)S(1)} collective-permute-done((bf16[64,512]{1,0:T(8,128)(2,1)S(1)}, bf16[64,512]{1,0:T(8,128)(2,1)S(1)}, u32[]{:S(2)}, u32[]{:S(2)}) %collective-permute-start.6) | collective-permute-done | bytes 65568 | tf_op jit(solution)/shard_map/ppermute | solution.py:301
  25.4 1.5 %collective-permute-done.7.refs_7_ = bf16[64,512]{1,0:T(8,128)(2,1)S(1)} collective-permute-done((bf16[64,512]{1,0:T(8,128)(2,1)S(1)}, bf16[64,512]{1,0:T(8,128)(2,1)S(1)}, u32[]{:S(2)}, u32[]{:S(2)}) %collective-permute-start.7) | collective-permute-done | bytes 65568 | tf_op jit(solution)/shard_map/ppermute | solution.py:301
  27.0 5.5 %patch_attention_and_ffn.3 = (bf16[64,512]{1,0:T(8,128)(2,1)S(1)}, bf16[64,512]{1,0:T(8,128)(2,1)S(1)}, bf16[64,512]{1,0:T(8,128)(2,1)S(1)}, bf16[64,512]{1,0:T(8,128)(2,1)S(1)}) custom-call(s32[3]{0:T(128)S(1)} %pad_add_fusion.place_ref, s32[2,2]{1,0:T(2,128)S(1)} %copy-done.8, bf16[64,512]{1,0:T(8,128)(2,1)S(1)} %get-tuple-element.39.refs_0_, ...), custom_call_target="tpu_custom_call" | custom-call | flops 5368709120 | bytes 1048576 | tf_op jit(solution)/shard_map/patch_attention_and_ffn/pallas_call | solution.py:265
  32.6 2.0 %collective-permute-start.9 = (bf16[64,512]{1,0:T(8,128)(2,1)S(1)}, bf16[64,512]{1,0:T(8,128)(2,1)S(1)}, u32[]{:S(2)}, u32[]{:S(2)}) collective-permute-start(bf16[64,512]{1,0:T(8,128)(2,1)S(1)} %get-tuple-element.44), channel_id=1, source_target_pairs={{0,20},{2,22},{4,16},{6,18},{8,28},{10,30},{12,24},{14,26},{16,4},... | collective-permute-start | bytes 196616 | tf_op jit(solution)/shard_map/ppermute | solution.py:311
  34.6 2.7 %collective-permute-start.10 = (bf16[64,512]{1,0:T(8,128)(2,1)S(1)}, bf16[64,512]{1,0:T(8,128)(2,1)S(1)}, u32[]{:S(2)}, u32[]{:S(2)}) collective-permute-start(bf16[64,512]{1,0:T(8,128)(2,1)S(1)} %get-tuple-element.45), channel_id=1, source_target_pairs={{0,24},{2,26},{4,28},{6,30},{8,16},{10,18},{12,20},{14,22},{16,8},... | collective-permute-start | bytes 196616 | tf_op jit(solution)/shard_map/ppermute | solution.py:311
  37.3 2.0 %collective-permute-start.11 = (bf16[64,512]{1,0:T(8,128)(2,1)S(1)}, bf16[64,512]{1,0:T(8,128)(2,1)S(1)}, u32[]{:S(2)}, u32[]{:S(2)}) collective-permute-start(bf16[64,512]{1,0:T(8,128)(2,1)S(1)} %get-tuple-element.46), channel_id=1, source_target_pairs={{0,28},{2,30},{4,24},{6,26},{8,20},{10,22},{12,16},{14,18},{16,12}... | collective-permute-start | bytes 196616 | tf_op jit(solution)/shard_map/ppermute | solution.py:311
  40.6 3.6 %collective-permute-done.11.refs_5_ = bf16[64,512]{1,0:T(8,128)(2,1)S(1)} collective-permute-done((bf16[64,512]{1,0:T(8,128)(2,1)S(1)}, bf16[64,512]{1,0:T(8,128)(2,1)S(1)}, u32[]{:S(2)}, u32[]{:S(2)}) %collective-permute-start.11) | collective-permute-done | bytes 65568 | tf_op jit(solution)/shard_map/ppermute | solution.py:311
  45.5 3.5 %time_attention.4 = (bf16[64,512]{1,0:T(8,128)(2,1)S(1)}, bf16[64,512]{1,0:T(8,128)(2,1)S(1)}, bf16[64,512]{1,0:T(8,128)(2,1)S(1)}, bf16[64,512]{1,0:T(8,128)(2,1)S(1)}) custom-call(s32[3]{0:T(128)S(1)} %pad_add_fusion.place_ref, bf16[2,256,512]{2,1,0:T(8,128)(2,1)S(1)} %bitcast.7, bf16[2,256,512]{2,1,0:T(8,128)(2,1)S(1)} %collective-permute-done.refs_1_, ...), custom_call_target="tpu_custom_call" | custom-call | flops 5368709120 | bytes 1048576 | tf_op jit(solution)/shard_map/time_attention/pallas_call | solution.py:251
  49.2 1.7 %collective-permute-start.17 = (bf16[64,512]{1,0:T(8,128)(2,1)S(1)}, bf16[64,512]{1,0:T(8,128)(2,1)S(1)}, u32[]{:S(2)}, u32[]{:S(2)}) collective-permute-start(bf16[64,512]{1,0:T(8,128)(2,1)S(1)} %get-tuple-element.49), channel_id=1, source_target_pairs={{0,8},{2,10},{4,12},{6,14},{8,0},{10,2},{12,4},{14,6},{1,9},{3,11}... | collective-permute-start | bytes 196616 | tf_op jit(solution)/shard_map/ppermute | solution.py:301
  50.9 2.6 %collective-permute-start.18 = (bf16[64,512]{1,0:T(8,128)(2,1)S(1)}, bf16[64,512]{1,0:T(8,128)(2,1)S(1)}, u32[]{:S(2)}, u32[]{:S(2)}) collective-permute-start(bf16[64,512]{1,0:T(8,128)(2,1)S(1)} %get-tuple-element.50), channel_id=1, source_target_pairs={{0,12},{2,14},{4,8},{6,10},{8,4},{10,6},{12,0},{14,2},{1,13},{3,15... | collective-permute-start | bytes 196616 | tf_op jit(solution)/shard_map/ppermute | solution.py:301
  55.6 2.2 %collective-permute-done.17.refs_2_ = bf16[64,512]{1,0:T(8,128)(2,1)S(1)} collective-permute-done((bf16[64,512]{1,0:T(8,128)(2,1)S(1)}, bf16[64,512]{1,0:T(8,128)(2,1)S(1)}, u32[]{:S(2)}, u32[]{:S(2)}) %collective-permute-start.17) | collective-permute-done | bytes 65568 | tf_op jit(solution)/shard_map/ppermute | solution.py:301
  59.8 2.2 %collective-permute-done.21.refs_6_ = bf16[64,512]{1,0:T(8,128)(2,1)S(1)} collective-permute-done((bf16[64,512]{1,0:T(8,128)(2,1)S(1)}, bf16[64,512]{1,0:T(8,128)(2,1)S(1)}, u32[]{:S(2)}, u32[]{:S(2)}) %collective-permute-start.21) | collective-permute-done | bytes 65568 | tf_op jit(solution)/shard_map/ppermute | solution.py:301
  62.8 5.7 %patch_attention_and_ffn.4 = (bf16[64,512]{1,0:T(8,128)(2,1)S(1)}, bf16[64,512]{1,0:T(8,128)(2,1)S(1)}, bf16[64,512]{1,0:T(8,128)(2,1)S(1)}, bf16[64,512]{1,0:T(8,128)(2,1)S(1)}) custom-call(s32[3]{0:T(128)S(1)} %pad_add_fusion.place_ref, s32[2,2]{1,0:T(2,128)S(1)} %copy-done.8, bf16[64,512]{1,0:T(8,128)(2,1)S(1)} %get-tuple-element.47.refs_0_, ...), custom_call_target="tpu_custom_call" | custom-call | flops 5368709120 | bytes 1048576 | tf_op jit(solution)/shard_map/patch_attention_and_ffn/pallas_call | solution.py:265
  68.5 1.7 %collective-permute-start.23 = (bf16[64,512]{1,0:T(8,128)(2,1)S(1)}, bf16[64,512]{1,0:T(8,128)(2,1)S(1)}, u32[]{:S(2)}, u32[]{:S(2)}) collective-permute-start(bf16[64,512]{1,0:T(8,128)(2,1)S(1)} %get-tuple-element.51), channel_id=1, source_target_pairs={{0,16},{2,18},{4,20},{6,22},{8,24},{10,26},{12,28},{14,30},{16,0},... | collective-permute-start | bytes 196616 | tf_op jit(solution)/shard_map/ppermute | solution.py:311
  70.5 2.3 %collective-permute-start.25 = (bf16[64,512]{1,0:T(8,128)(2,1)S(1)}, bf16[64,512]{1,0:T(8,128)(2,1)S(1)}, u32[]{:S(2)}, u32[]{:S(2)}) collective-permute-start(bf16[64,512]{1,0:T(8,128)(2,1)S(1)} %get-tuple-element.53), channel_id=1, source_target_pairs={{0,24},{2,26},{4,28},{6,30},{8,16},{10,18},{12,20},{14,22},{16,8},... | collective-permute-start | bytes 196616 | tf_op jit(solution)/shard_map/ppermute | solution.py:311
  72.9 2.4 %collective-permute-start.26 = (bf16[64,512]{1,0:T(8,128)(2,1)S(1)}, bf16[64,512]{1,0:T(8,128)(2,1)S(1)}, u32[]{:S(2)}, u32[]{:S(2)}) collective-permute-start(bf16[64,512]{1,0:T(8,128)(2,1)S(1)} %get-tuple-element.54), channel_id=1, source_target_pairs={{0,28},{2,30},{4,24},{6,26},{8,20},{10,22},{12,16},{14,18},{16,12}... | collective-permute-start | bytes 196616 | tf_op jit(solution)/shard_map/ppermute | solution.py:311
  76.8 3.0 %collective-permute-done.26.refs_3_ = bf16[64,512]{1,0:T(8,128)(2,1)S(1)} collective-permute-done((bf16[64,512]{1,0:T(8,128)(2,1)S(1)}, bf16[64,512]{1,0:T(8,128)(2,1)S(1)}, u32[]{:S(2)}, u32[]{:S(2)}) %collective-permute-start.26) | collective-permute-done | bytes 65568 | tf_op jit(solution)/shard_map/ppermute | solution.py:311
  81.7 3.2 %collective-permute-start.32 = (bf16[64,512]{1,0:T(8,128)(2,1)S(1)}, bf16[64,512]{1,0:T(8,128)(2,1)S(1)}, u32[]{:S(2)}, u32[]{:S(2)}) collective-permute-start(bf16[64,512]{1,0:T(8,128)(2,1)S(1)} %get-tuple-element.57), channel_id=1, source_target_pairs={{0,8},{2,10},{4,12},{6,14},{8,0},{10,2},{12,4},{14,6},{1,9},{3,11}... | collective-permute-start | bytes 196616 | tf_op jit(solution)/shard_map/ppermute | solution.py:301
  93.5 1.8 %collective-permute-done.37.refs_7_ = bf16[64,512]{1,0:T(8,128)(2,1)S(1)} collective-permute-done((bf16[64,512]{1,0:T(8,128)(2,1)S(1)}, bf16[64,512]{1,0:T(8,128)(2,1)S(1)}, u32[]{:S(2)}, u32[]{:S(2)}) %collective-permute-start.37) | collective-permute-done | bytes 65568 | tf_op jit(solution)/shard_map/ppermute | solution.py:301
  95.9 8.6 %collective-permute-start.39 = (bf16[256,512]{1,0:T(8,128)(2,1)S(1)}, bf16[256,512]{1,0:T(8,128)(2,1)S(1)}, u32[]{:S(2)}, u32[]{:S(2)}) collective-permute-start(bf16[256,512]{1,0:T(8,128)(2,1)S(1)} %patch_attention_and_ffn.5.refs_0_), channel_id=1, source_target_pairs={{0,16},{16,0},{1,17},{17,1},{2,18},{18,2},{3,19},{19,3},{4,20},{20... | collective-permute-start | bytes 786440 | tf_op jit(solution)/shard_map/ppermute | solution.py:343
  104.5 4.5 %collective-permute-done.39.refs_1_ = bf16[256,512]{1,0:T(8,128)(2,1)S(1)} collective-permute-done((bf16[256,512]{1,0:T(8,128)(2,1)S(1)}, bf16[256,512]{1,0:T(8,128)(2,1)S(1)}, u32[]{:S(2)}, u32[]{:S(2)}) %collective-permute-start.39) | collective-permute-done | bytes 262176 | tf_op jit(solution)/shard_map/ppermute | solution.py:343
  109.6 1.5 %collective-permute-start.40 = (bf16[64,512]{1,0:T(8,128)(2,1)S(1)}, bf16[64,512]{1,0:T(8,128)(2,1)S(1)}, u32[]{:S(2)}, u32[]{:S(2)}) collective-permute-start(bf16[64,512]{1,0:T(8,128)(2,1)S(1)} %get-tuple-element.70), channel_id=1, source_target_pairs={{0,4},{2,6},{4,0},{6,2},{8,12},{10,14},{12,8},{14,10},{1,5},{3,7},... | collective-permute-start | bytes 196616 | tf_op jit(solution)/shard_map/ppermute | solution.py:301
  111.1 2.3 %collective-permute-start.41 = (bf16[64,512]{1,0:T(8,128)(2,1)S(1)}, bf16[64,512]{1,0:T(8,128)(2,1)S(1)}, u32[]{:S(2)}, u32[]{:S(2)}) collective-permute-start(bf16[64,512]{1,0:T(8,128)(2,1)S(1)} %get-tuple-element.71), channel_id=1, source_target_pairs={{0,8},{2,10},{4,12},{6,14},{8,0},{10,2},{12,4},{14,6},{1,9},{3,11}... | collective-permute-start | bytes 196616 | tf_op jit(solution)/shard_map/ppermute | solution.py:301
  115.0 2.0 %collective-permute-done.41.refs_4_ = bf16[64,512]{1,0:T(8,128)(2,1)S(1)} collective-permute-done((bf16[64,512]{1,0:T(8,128)(2,1)S(1)}, bf16[64,512]{1,0:T(8,128)(2,1)S(1)}, u32[]{:S(2)}, u32[]{:S(2)}) %collective-permute-start.41) | collective-permute-done | bytes 65568 | tf_op jit(solution)/shard_map/ppermute | solution.py:301
  117.0 2.5 %collective-permute-done.42.refs_5_ = bf16[64,512]{1,0:T(8,128)(2,1)S(1)} collective-permute-done((bf16[64,512]{1,0:T(8,128)(2,1)S(1)}, bf16[64,512]{1,0:T(8,128)(2,1)S(1)}, u32[]{:S(2)}, u32[]{:S(2)}) %collective-permute-start.42) | collective-permute-done | bytes 65568 | tf_op jit(solution)/shard_map/ppermute | solution.py:301
  119.5 1.9 %final_order.1 = bf16[2,256,512]{2,1,0:T(8,128)(2,1)} custom-call(s32[3]{0:T(128)S(1)} %pad_add_fusion.place_ref, bf16[256,512]{1,0:T(8,128)(2,1)S(1)} %constant_dynamic-update-slice_fusion.refs_0_, bf16[256,512]{1,0:T(8,128)(2,1)S(1)} %collective-permute-done.38.refs_1_, bf16[64,512]{1,0:T(8,128)(2,1)S(1)} %get-tuple-element.69.refs_2_, ...), custom_call_target="tpu_custom_call" | custom-call | tf_op jit(solution)/shard_map/final_order/pallas_call | solution.py:290
  (90 shorter events, 30.8 us)
Async XLA Ops:
  10.6 7.3 %collective-permute-start.1 = (bf16[64,512]{1,0:T(8,128)(2,1)S(1)}, bf16[64,512]{1,0:T(8,128)(2,1)S(1)}, u32[]{:S(2)}, u32[]{:S(2)}) collective-permute-start(bf16[64,512]{1,0:T(8,128)(2,1)S(1)} %get-tuple-element.40), channel_id=1, source_target_pairs={{0,4},{2,6},{4,0},{6,2},{8,12},{10,14},{12,8},{14,10},{1,5},{3,7},... | collective-permute-start | bytes 196616 | tf_op jit(solution)/shard_map/ppermute | solution.py:301
  13.6 7.5 %collective-permute-start.2 = (bf16[64,512]{1,0:T(8,128)(2,1)S(1)}, bf16[64,512]{1,0:T(8,128)(2,1)S(1)}, u32[]{:S(2)}, u32[]{:S(2)}) collective-permute-start(bf16[64,512]{1,0:T(8,128)(2,1)S(1)} %get-tuple-element.41), channel_id=1, source_target_pairs={{0,8},{2,10},{4,12},{6,14},{8,0},{10,2},{12,4},{14,6},{1,9},{3,11}... | collective-permute-start | bytes 196616 | tf_op jit(solution)/shard_map/ppermute | solution.py:301
  16.2 6.4 %collective-permute-start.3 = (bf16[64,512]{1,0:T(8,128)(2,1)S(1)}, bf16[64,512]{1,0:T(8,128)(2,1)S(1)}, u32[]{:S(2)}, u32[]{:S(2)}) collective-permute-start(bf16[64,512]{1,0:T(8,128)(2,1)S(1)} %get-tuple-element.42), channel_id=1, source_target_pairs={{0,12},{2,14},{4,8},{6,10},{8,4},{10,6},{12,0},{14,2},{1,13},{3,15... | collective-permute-start | bytes 196616 | tf_op jit(solution)/shard_map/ppermute | solution.py:301
  16.2 7.7 %collective-permute-start.4 = (bf16[64,512]{1,0:T(8,128)(2,1)S(1)}, bf16[64,512]{1,0:T(8,128)(2,1)S(1)}, u32[]{:S(2)}, u32[]{:S(2)}) collective-permute-start(bf16[64,512]{1,0:T(8,128)(2,1)S(1)} %get-tuple-element.39.refs_0_), channel_id=1, source_target_pairs={{0,2},{2,0},{4,6},{6,4},{8,10},{10,8},{12,14},{14,12},{1,3},{3,1},... | collective-permute-start | bytes 196616 | tf_op jit(solution)/shard_map/ppermute | solution.py:301
  17.9 6.0 %collective-permute-start.5 = (bf16[64,512]{1,0:T(8,128)(2,1)S(1)}, bf16[64,512]{1,0:T(8,128)(2,1)S(1)}, u32[]{:S(2)}, u32[]{:S(2)}) collective-permute-start(bf16[64,512]{1,0:T(8,128)(2,1)S(1)} %collective-permute-done.1.refs_1_), channel_id=1, source_target_pairs={{0,2},{2,0},{4,6},{6,4},{8,10},{10,8},{12,14},{14,12},{1,3},{3,1},... | collective-permute-start | bytes 196616 | tf_op jit(solution)/shard_map/ppermute | solution.py:301
  32.5 6.8 %collective-permute-start.8 = (bf16[64,512]{1,0:T(8,128)(2,1)S(1)}, bf16[64,512]{1,0:T(8,128)(2,1)S(1)}, u32[]{:S(2)}, u32[]{:S(2)}) collective-permute-start(bf16[64,512]{1,0:T(8,128)(2,1)S(1)} %get-tuple-element.43), channel_id=1, source_target_pairs={{0,16},{2,18},{4,20},{6,22},{8,24},{10,26},{12,28},{14,30},{16,0},... | collective-permute-start | bytes 196616 | tf_op jit(solution)/shard_map/ppermute | solution.py:311
  32.6 6.7 %collective-permute-start.9 = (bf16[64,512]{1,0:T(8,128)(2,1)S(1)}, bf16[64,512]{1,0:T(8,128)(2,1)S(1)}, u32[]{:S(2)}, u32[]{:S(2)}) collective-permute-start(bf16[64,512]{1,0:T(8,128)(2,1)S(1)} %get-tuple-element.44), channel_id=1, source_target_pairs={{0,20},{2,22},{4,16},{6,18},{8,28},{10,30},{12,24},{14,26},{16,4},... | collective-permute-start | bytes 196616 | tf_op jit(solution)/shard_map/ppermute | solution.py:311
  34.6 6.1 %collective-permute-start.10 = (bf16[64,512]{1,0:T(8,128)(2,1)S(1)}, bf16[64,512]{1,0:T(8,128)(2,1)S(1)}, u32[]{:S(2)}, u32[]{:S(2)}) collective-permute-start(bf16[64,512]{1,0:T(8,128)(2,1)S(1)} %get-tuple-element.45), channel_id=1, source_target_pairs={{0,24},{2,26},{4,28},{6,30},{8,16},{10,18},{12,20},{14,22},{16,8},... | collective-permute-start | bytes 196616 | tf_op jit(solution)/shard_map/ppermute | solution.py:311
  37.3 7.0 %collective-permute-start.11 = (bf16[64,512]{1,0:T(8,128)(2,1)S(1)}, bf16[64,512]{1,0:T(8,128)(2,1)S(1)}, u32[]{:S(2)}, u32[]{:S(2)}) collective-permute-start(bf16[64,512]{1,0:T(8,128)(2,1)S(1)} %get-tuple-element.46), channel_id=1, source_target_pairs={{0,28},{2,30},{4,24},{6,26},{8,20},{10,22},{12,16},{14,18},{16,12}... | collective-permute-start | bytes 196616 | tf_op jit(solution)/shard_map/ppermute | solution.py:311
  39.3 5.0 %collective-permute-start.12 = (bf16[64,512]{1,0:T(8,128)(2,1)S(1)}, bf16[64,512]{1,0:T(8,128)(2,1)S(1)}, u32[]{:S(2)}, u32[]{:S(2)}) collective-permute-start(bf16[64,512]{1,0:T(8,128)(2,1)S(1)} %collective-permute-done.8.refs_2_), channel_id=1, source_target_pairs={{0,1},{1,0},{2,3},{3,2},{4,5},{5,4},{6,7},{7,6},{8,9},{9,8},{10,11... | collective-permute-start | bytes 196616 | tf_op jit(solution)/shard_map/ppermute | solution.py:301
  39.3 5.0 %collective-permute-start.13 = (bf16[64,512]{1,0:T(8,128)(2,1)S(1)}, bf16[64,512]{1,0:T(8,128)(2,1)S(1)}, u32[]{:S(2)}, u32[]{:S(2)}) collective-permute-start(bf16[64,512]{1,0:T(8,128)(2,1)S(1)} %collective-permute-done.9.refs_3_), channel_id=1, source_target_pairs={{0,1},{1,0},{2,3},{3,2},{4,5},{5,4},{6,7},{7,6},{8,9},{9,8},{10,11... | collective-permute-start | bytes 196616 | tf_op jit(solution)/shard_map/ppermute | solution.py:301
  49.1 5.2 %collective-permute-start.16 = (bf16[64,512]{1,0:T(8,128)(2,1)S(1)}, bf16[64,512]{1,0:T(8,128)(2,1)S(1)}, u32[]{:S(2)}, u32[]{:S(2)}) collective-permute-start(bf16[64,512]{1,0:T(8,128)(2,1)S(1)} %get-tuple-element.48), channel_id=1, source_target_pairs={{0,4},{2,6},{4,0},{6,2},{8,12},{10,14},{12,8},{14,10},{1,5},{3,7},... | collective-permute-start | bytes 196616 | tf_op jit(solution)/shard_map/ppermute | solution.py:301
  49.2 8.6 %collective-permute-start.17 = (bf16[64,512]{1,0:T(8,128)(2,1)S(1)}, bf16[64,512]{1,0:T(8,128)(2,1)S(1)}, u32[]{:S(2)}, u32[]{:S(2)}) collective-permute-start(bf16[64,512]{1,0:T(8,128)(2,1)S(1)} %get-tuple-element.49), channel_id=1, source_target_pairs={{0,8},{2,10},{4,12},{6,14},{8,0},{10,2},{12,4},{14,6},{1,9},{3,11}... | collective-permute-start | bytes 196616 | tf_op jit(solution)/shard_map/ppermute | solution.py:301
  50.9 7.6 %collective-permute-start.18 = (bf16[64,512]{1,0:T(8,128)(2,1)S(1)}, bf16[64,512]{1,0:T(8,128)(2,1)S(1)}, u32[]{:S(2)}, u32[]{:S(2)}) collective-permute-start(bf16[64,512]{1,0:T(8,128)(2,1)S(1)} %get-tuple-element.50), channel_id=1, source_target_pairs={{0,12},{2,14},{4,8},{6,10},{8,4},{10,6},{12,0},{14,2},{1,13},{3,15... | collective-permute-start | bytes 196616 | tf_op jit(solution)/shard_map/ppermute | solution.py:301
  53.5 6.3 %collective-permute-start.19 = (bf16[64,512]{1,0:T(8,128)(2,1)S(1)}, bf16[64,512]{1,0:T(8,128)(2,1)S(1)}, u32[]{:S(2)}, u32[]{:S(2)}) collective-permute-start(bf16[64,512]{1,0:T(8,128)(2,1)S(1)} %get-tuple-element.47.refs_0_), channel_id=1, source_target_pairs={{0,2},{2,0},{4,6},{6,4},{8,10},{10,8},{12,14},{14,12},{1,3},{3,1},... | collective-permute-start | bytes 196616 | tf_op jit(solution)/shard_map/ppermute | solution.py:301
  54.3 5.5 %collective-permute-start.20 = (bf16[64,512]{1,0:T(8,128)(2,1)S(1)}, bf16[64,512]{1,0:T(8,128)(2,1)S(1)}, u32[]{:S(2)}, u32[]{:S(2)}) collective-permute-start(bf16[64,512]{1,0:T(8,128)(2,1)S(1)} %collective-permute-done.16.refs_1_), channel_id=1, source_target_pairs={{0,2},{2,0},{4,6},{6,4},{8,10},{10,8},{12,14},{14,12},{1,3},{3,1},... | collective-permute-start | bytes 196616 | tf_op jit(solution)/shard_map/ppermute | solution.py:301
  68.5 6.8 %collective-permute-start.23 = (bf16[64,512]{1,0:T(8,128)(2,1)S(1)}, bf16[64,512]{1,0:T(8,128)(2,1)S(1)}, u32[]{:S(2)}, u32[]{:S(2)}) collective-permute-start(bf16[64,512]{1,0:T(8,128)(2,1)S(1)} %get-tuple-element.51), channel_id=1, source_target_pairs={{0,16},{2,18},{4,20},{6,22},{8,24},{10,26},{12,28},{14,30},{16,0},... | collective-permute-start | bytes 196616 | tf_op jit(solution)/shard_map/ppermute | solution.py:311
  70.2 5.2 %collective-permute-start.24 = (bf16[64,512]{1,0:T(8,128)(2,1)S(1)}, bf16[64,512]{1,0:T(8,128)(2,1)S(1)}, u32[]{:S(2)}, u32[]{:S(2)}) collective-permute-start(bf16[64,512]{1,0:T(8,128)(2,1)S(1)} %get-tuple-element.52), channel_id=1, source_target_pairs={{0,20},{2,22},{4,16},{6,18},{8,28},{10,30},{12,24},{14,26},{16,4},... | collective-permute-start | bytes 196616 | tf_op jit(solution)/shard_map/ppermute | solution.py:311
  70.5 6.2 %collective-permute-start.25 = (bf16[64,512]{1,0:T(8,128)(2,1)S(1)}, bf16[64,512]{1,0:T(8,128)(2,1)S(1)}, u32[]{:S(2)}, u32[]{:S(2)}) collective-permute-start(bf16[64,512]{1,0:T(8,128)(2,1)S(1)} %get-tuple-element.53), channel_id=1, source_target_pairs={{0,24},{2,26},{4,28},{6,30},{8,16},{10,18},{12,20},{14,22},{16,8},... | collective-permute-start | bytes 196616 | tf_op jit(solution)/shard_map/ppermute | solution.py:311
  72.9 7.0 %collective-permute-start.26 = (bf16[64,512]{1,0:T(8,128)(2,1)S(1)}, bf16[64,512]{1,0:T(8,128)(2,1)S(1)}, u32[]{:S(2)}, u32[]{:S(2)}) collective-permute-start(bf16[64,512]{1,0:T(8,128)(2,1)S(1)} %get-tuple-element.54), channel_id=1, source_target_pairs={{0,28},{2,30},{4,24},{6,26},{8,20},{10,22},{12,16},{14,18},{16,12}... | collective-permute-start | bytes 196616 | tf_op jit(solution)/shard_map/ppermute | solution.py:311
  75.3 5.0 %collective-permute-start.27 = (bf16[64,512]{1,0:T(8,128)(2,1)S(1)}, bf16[64,512]{1,0:T(8,128)(2,1)S(1)}, u32[]{:S(2)}, u32[]{:S(2)}) collective-permute-start(bf16[64,512]{1,0:T(8,128)(2,1)S(1)} %collective-permute-done.23.refs_0_), channel_id=1, source_target_pairs={{0,1},{1,0},{2,3},{3,2},{4,5},{5,4},{6,7},{7,6},{8,9},{9,8},{10,11... | collective-permute-start | bytes 196616 | tf_op jit(solution)/shard_map/ppermute | solution.py:301
  75.4 4.9 %collective-permute-start.28 = (bf16[64,512]{1,0:T(8,128)(2,1)S(1)}, bf16[64,512]{1,0:T(8,128)(2,1)S(1)}, u32[]{:S(2)}, u32[]{:S(2)}) collective-permute-start(bf16[64,512]{1,0:T(8,128)(2,1)S(1)} %collective-permute-done.24.refs_1_), channel_id=1, source_target_pairs={{0,1},{1,0},{2,3},{3,2},{4,5},{5,4},{6,7},{7,6},{8,9},{9,8},{10,11... | collective-permute-start | bytes 196616 | tf_op jit(solution)/shard_map/ppermute | solution.py:301
  79.9 15.5 %collective-permute-start.38 = (bf16[256,512]{1,0:T(8,128)(2,1)S(1)}, bf16[256,512]{1,0:T(8,128)(2,1)S(1)}, u32[]{:S(2)}, u32[]{:S(2)}) collective-permute-start(bf16[256,512]{1,0:T(8,128)(2,1)S(1)} %constant_dynamic-update-slice_fusion.refs_0_), channel_id=1, source_target_pairs={{0,16},{16,0},{1,17},{17,1},{2,18},{18,2},{3,19},{19,3},{4,20},{20... | collective-permute-start | bytes 786440 | tf_op jit(solution)/shard_map/ppermute | solution.py:343
  81.7 5.3 %collective-permute-start.31 = (bf16[64,512]{1,0:T(8,128)(2,1)S(1)}, bf16[64,512]{1,0:T(8,128)(2,1)S(1)}, u32[]{:S(2)}, u32[]{:S(2)}) collective-permute-start(bf16[64,512]{1,0:T(8,128)(2,1)S(1)} %get-tuple-element.56), channel_id=1, source_target_pairs={{0,4},{2,6},{4,0},{6,2},{8,12},{10,14},{12,8},{14,10},{1,5},{3,7},... | collective-permute-start | bytes 196616 | tf_op jit(solution)/shard_map/ppermute | solution.py:301
  81.7 7.3 %collective-permute-start.32 = (bf16[64,512]{1,0:T(8,128)(2,1)S(1)}, bf16[64,512]{1,0:T(8,128)(2,1)S(1)}, u32[]{:S(2)}, u32[]{:S(2)}) collective-permute-start(bf16[64,512]{1,0:T(8,128)(2,1)S(1)} %get-tuple-element.57), channel_id=1, source_target_pairs={{0,8},{2,10},{4,12},{6,14},{8,0},{10,2},{12,4},{14,6},{1,9},{3,11}... | collective-permute-start | bytes 196616 | tf_op jit(solution)/shard_map/ppermute | solution.py:301
  84.9 6.2 %collective-permute-start.33 = (bf16[64,512]{1,0:T(8,128)(2,1)S(1)}, bf16[64,512]{1,0:T(8,128)(2,1)S(1)}, u32[]{:S(2)}, u32[]{:S(2)}) collective-permute-start(bf16[64,512]{1,0:T(8,128)(2,1)S(1)} %get-tuple-element.58), channel_id=1, source_target_pairs={{0,12},{2,14},{4,8},{6,10},{8,4},{10,6},{12,0},{14,2},{1,13},{3,15... | collective-permute-start | bytes 196616 | tf_op jit(solution)/shard_map/ppermute | solution.py:301
  86.1 6.3 %collective-permute-start.34 = (bf16[64,512]{1,0:T(8,128)(2,1)S(1)}, bf16[64,512]{1,0:T(8,128)(2,1)S(1)}, u32[]{:S(2)}, u32[]{:S(2)}) collective-permute-start(bf16[64,512]{1,0:T(8,128)(2,1)S(1)} %get-tuple-element.61.refs_0_), channel_id=1, source_target_pairs={{0,2},{2,0},{4,6},{6,4},{8,10},{10,8},{12,14},{14,12},{1,3},{3,1},... | collective-permute-start | bytes 196616 | tf_op jit(solution)/shard_map/ppermute | solution.py:301
  87.0 5.5 %collective-permute-start.35 = (bf16[64,512]{1,0:T(8,128)(2,1)S(1)}, bf16[64,512]{1,0:T(8,128)(2,1)S(1)}, u32[]{:S(2)}, u32[]{:S(2)}) collective-permute-start(bf16[64,512]{1,0:T(8,128)(2,1)S(1)} %collective-permute-done.31.refs_1_), channel_id=1, source_target_pairs={{0,2},{2,0},{4,6},{6,4},{8,10},{10,8},{12,14},{14,12},{1,3},{3,1},... | collective-permute-start | bytes 196616 | tf_op jit(solution)/shard_map/ppermute | solution.py:301
  95.9 13.1 %collective-permute-start.39 = (bf16[256,512]{1,0:T(8,128)(2,1)S(1)}, bf16[256,512]{1,0:T(8,128)(2,1)S(1)}, u32[]{:S(2)}, u32[]{:S(2)}) collective-permute-start(bf16[256,512]{1,0:T(8,128)(2,1)S(1)} %patch_attention_and_ffn.5.refs_0_), channel_id=1, source_target_pairs={{0,16},{16,0},{1,17},{17,1},{2,18},{18,2},{3,19},{19,3},{4,20},{20... | collective-permute-start | bytes 786440 | tf_op jit(solution)/shard_map/ppermute | solution.py:343
  109.6 5.4 %collective-permute-start.40 = (bf16[64,512]{1,0:T(8,128)(2,1)S(1)}, bf16[64,512]{1,0:T(8,128)(2,1)S(1)}, u32[]{:S(2)}, u32[]{:S(2)}) collective-permute-start(bf16[64,512]{1,0:T(8,128)(2,1)S(1)} %get-tuple-element.70), channel_id=1, source_target_pairs={{0,4},{2,6},{4,0},{6,2},{8,12},{10,14},{12,8},{14,10},{1,5},{3,7},... | collective-permute-start | bytes 196616 | tf_op jit(solution)/shard_map/ppermute | solution.py:301
  111.1 5.9 %collective-permute-start.41 = (bf16[64,512]{1,0:T(8,128)(2,1)S(1)}, bf16[64,512]{1,0:T(8,128)(2,1)S(1)}, u32[]{:S(2)}, u32[]{:S(2)}) collective-permute-start(bf16[64,512]{1,0:T(8,128)(2,1)S(1)} %get-tuple-element.71), channel_id=1, source_target_pairs={{0,8},{2,10},{4,12},{6,14},{8,0},{10,2},{12,4},{14,6},{1,9},{3,11}... | collective-permute-start | bytes 196616 | tf_op jit(solution)/shard_map/ppermute | solution.py:301
  113.4 6.1 %collective-permute-start.42 = (bf16[64,512]{1,0:T(8,128)(2,1)S(1)}, bf16[64,512]{1,0:T(8,128)(2,1)S(1)}, u32[]{:S(2)}, u32[]{:S(2)}) collective-permute-start(bf16[64,512]{1,0:T(8,128)(2,1)S(1)} %get-tuple-element.72), channel_id=1, source_target_pairs={{0,12},{2,14},{4,8},{6,10},{8,4},{10,6},{12,0},{14,2},{1,13},{3,15... | collective-permute-start | bytes 196616 | tf_op jit(solution)/shard_map/ppermute | solution.py:301
  (22 other events, 200.6 us)
